TPU v7x, 128 devices: a whole 4x4x4 slice. The times are simulated.
128 devices in a mesh: segment: 8 (over x, core), dp: 16 (over z, y).
Axes of the slice: x: 4, y: 4, z: 4, core: 2. Of those that a mesh axis runs over, the one named last changes fastest.
Arguments:
- embeds: bfloat16 [2, 16, 128, 4096], P(None, 'dp'), may hold values from -6 to 6
- base_weight: bfloat16 [8, 4096, 4096], P('segment', 'dp'), may hold values from -0.09375 to 0.09375
- norm_gain: float32 [8, 4096], P('segment'), may hold values from 0.25 to 1.75
- skill_down: bfloat16 [8, 16, 8, 4096], P('segment'), may hold values from -0.09375 to 0.09375
- skill_up: bfloat16 [8, 16, 8, 4096], P('segment'), may hold values from -2 to 2
- task_ids: int32 [2, 16], replicated, may hold values from 0 to 1835
- allocation: int32 [1836, 16], replicated, may hold values 0 or 1
- target_lengths: int32 [2, 16], replicated, may hold values from 1 to 128
- cotangent: bfloat16 [2, 16, 128, 4096], P(None, 'dp'), may hold values from -6 to 6
Outputs:
- hidden: bfloat16 [8, 2, 16, 128, 4096], P('segment', None, 'dp')
- input_grads: bfloat16 [8, 2, 16, 128, 4096], P('segment', None, 'dp')
- grad_down: float32 [8, 16, 8, 4096], P('segment', None, None, 'dp')
- grad_up: float32 [8, 16, 8, 4096], P('segment', None, None, 'dp')
All inputs are finite; a program needn't handle non-finite values.
Results may differ from a plain program's by a relative error of at most 0.019.
Values may be sent and summed in bfloat16 or wider, within the bound.
A program may use at most 192 MiB of HBM per device.

v0:
```python
import jax
import jax.numpy as jnp
from jax import lax
from jax.sharding import PartitionSpec as P

EPS = 1e-06


def shifted(block, axis, distance):
    devices = range(lax.axis_size(axis))
    route = [(i - distance, i) for i in devices if i - distance in devices]
    return lax.ppermute(block, axis, route)


def in_blocks(x, dim, size):
    before, after = (x.shape[:dim], x.shape[dim + 1 :])
    return jnp.moveaxis(x.reshape(*before, size, -1, *after), dim, 0)


def sent_and_summed(x, axis, dim):
    size = lax.axis_size(axis)
    parts = lax.all_to_all(in_blocks(x, dim, size), axis, 0, 0, tiled=True)
    return jnp.sum(parts.astype(jnp.float32), axis=0)


def side_by_side(arrays, axis, dim, along):
    both = jnp.concatenate(arrays, axis=along)
    result, at, done = (sent_and_summed(both, axis, dim), 0, [])
    for a in arrays:
        done.append(lax.slice_in_dim(result, at, at + a.shape[along], axis=along))
        at += a.shape[along]
    return tuple(done)


def prepare(x, gain, down_t):
    xf = x.astype(jnp.float32)
    inv = lax.rsqrt(jnp.mean(xf * xf, axis=-1, keepdims=True) + EPS)
    normed = (xf * inv * gain).astype(jnp.bfloat16)
    low = jnp.dot(normed, down_t.T, preferred_element_type=jnp.float32).astype(jnp.bfloat16)
    return (normed, low, inv)


def forward_full(x, weight, gain, down_t, up_t):
    normed, low, inv = prepare(x, gain, down_t)
    total = x.astype(jnp.float32) + jnp.dot(normed, weight, preferred_element_type=jnp.float32)
    total = total + jnp.dot(low, up_t, preferred_element_type=jnp.float32)
    return (total.astype(jnp.bfloat16), normed, low, inv)


def backward_core(x, normed, low, inv, grad_out, weight, gain, down_t, up_t):
    g_low = jnp.dot(grad_out, up_t.T, preferred_element_type=jnp.float32).astype(jnp.bfloat16)
    dnorm = jnp.dot(grad_out, weight.T, preferred_element_type=jnp.float32)
    dnorm = dnorm + jnp.dot(g_low, down_t, preferred_element_type=jnp.float32)
    seq_down = jnp.dot(g_low.T, normed, preferred_element_type=jnp.float32)
    seq_up = jnp.dot(low.T, grad_out, preferred_element_type=jnp.float32)
    xf = x.astype(jnp.float32)
    scaled = gain * dnorm
    grad_in = (
        grad_out.astype(jnp.float32)
        + inv * scaled
        - xf * inv * inv * inv * jnp.mean(xf * scaled, axis=-1, keepdims=True)
    )
    return (grad_in.astype(jnp.bfloat16), seq_down, seq_up)


def pick(table, index):
    return lax.dynamic_index_in_dim(table, index, 0, keepdims=False)


def place(table, value, index, active):
    return jnp.where(active, lax.dynamic_update_index_in_dim(table, value, index, 0), table)


def shards(
    embeds,
    base_weight,
    norm_gain,
    skill_down,
    skill_up,
    task_ids,
    allocation,
    target_lengths,
    cotangent,
):
    segments = lax.axis_size("segment")
    segment = lax.axis_index("segment")
    member = lax.axis_index("dp")
    weight = lax.all_gather(base_weight[0], "dp", axis=0, tiled=True)
    gain = norm_gain[0]
    micro = embeds.shape[0]
    rows = embeds.shape[2]
    width = embeds.shape[3]
    splits = 1
    blocks = micro * splits
    block_rows = rows // splits
    tasks = lax.dynamic_index_in_dim(task_ids, member, 1, keepdims=False)
    lengths = lax.dynamic_index_in_dim(target_lengths, member, 1, keepdims=False)
    onehot = (tasks[:, None] == jnp.arange(allocation.shape[0], dtype=jnp.int32)[None, :]).astype(
        jnp.float32
    )
    alloc = allocation.astype(jnp.float32)
    counts = jnp.maximum(jnp.sum(alloc, axis=1, keepdims=True), 1.0)
    mix = jnp.einsum("mt,ts->ms", onehot, alloc / counts, precision=lax.Precision.HIGHEST)
    down_seq = jnp.einsum(
        "ms,srd->mrd", mix, skill_down[0].astype(jnp.float32), precision=lax.Precision.HIGHEST
    ).astype(jnp.bfloat16)
    up_seq = jnp.einsum(
        "ms,srd->mrd", mix, skill_up[0].astype(jnp.float32), precision=lax.Precision.HIGHEST
    ).astype(jnp.bfloat16)
    down_all = jnp.repeat(down_seq, splits, axis=0)
    up_all = jnp.repeat(up_seq, splits, axis=0)
    mix_all = jnp.repeat(mix, splits, axis=0)
    firsts = embeds[:, 0]
    live = jnp.arange(rows, dtype=jnp.int32)[None, :] < lengths[:, None]
    seeds = cotangent[:, 0] * live[..., None].astype(jnp.bfloat16)
    ticks = segments + blocks - 1
    rank = down_all.shape[1]
    blank = jnp.zeros((block_rows, width), jnp.bfloat16)
    stack_blank = jnp.zeros((blocks, block_rows, width), jnp.bfloat16)
    low_blank = jnp.zeros((blocks, block_rows, rank), jnp.bfloat16)
    inv_blank = jnp.zeros((blocks, block_rows, 1), jnp.float32)

    def forward_tick(tick, carry):
        incoming, saved, outs, kept_norm, kept_low, kept_inv = carry
        slot = tick - segment
        active = (slot >= 0) & (slot < blocks)
        index = jnp.clip(slot, 0, blocks - 1)
        x = jnp.where(segment == 0, pick(firsts, index), incoming)
        result, normed, low, inv = lax.cond(
            active,
            lambda: forward_full(x, weight, gain, pick(down_all, index), pick(up_all, index)),
            lambda: (
                blank,
                blank,
                jnp.zeros((block_rows, rank), jnp.bfloat16),
                jnp.zeros((block_rows, 1), jnp.float32),
            ),
        )
        saved = place(saved, x, index, active)
        outs = place(outs, result, index, active)
        return (result, (saved, outs, kept_norm, kept_low, kept_inv))

    def forward_step(tick, carry):
        result, rest = forward_tick(tick, carry)
        moved = shifted(result, "segment", 1)
        return (moved,) + rest

    carry = (blank, stack_blank, stack_blank, stack_blank, low_blank, inv_blank)
    carry = lax.fori_loop(0, ticks - 1, forward_step, carry)
    _, (saved, outs, kept_norm, kept_low, kept_inv) = forward_tick(ticks - 1, carry)
    skills = skill_down.shape[1]
    acc_blank = jnp.zeros((skills, rank, width), jnp.float32)

    def backward_tick(tick, carry):
        incoming, grads_in, acc_down, acc_up = carry
        slot = tick - (segments - 1 - segment)
        active = (slot >= 0) & (slot < blocks)
        index = jnp.clip(slot, 0, blocks - 1)
        grad_out = jnp.where(segment == segments - 1, pick(seeds, index), incoming)
        x = pick(saved, index)
        down_t = pick(down_all, index)
        up_t = pick(up_all, index)

        def run():
            normed, low, inv = prepare(x, gain, down_t)
            return backward_core(x, normed, low, inv, grad_out, weight, gain, down_t, up_t)

        grad_in, seq_down, seq_up = lax.cond(
            active,
            run,
            lambda: (
                blank,
                jnp.zeros((rank, width), jnp.float32),
                jnp.zeros((rank, width), jnp.float32),
            ),
        )
        weights = pick(mix_all, index)[:, None, None]
        acc_down = acc_down + weights * seq_down[None]
        acc_up = acc_up + weights * seq_up[None]
        grads_in = place(grads_in, grad_in, index, active)
        return (grad_in, (grads_in, acc_down, acc_up))

    def backward_step(tick, carry):
        grad_in, rest = backward_tick(tick, carry)
        moved = shifted(grad_in, "segment", -1)
        return (moved,) + rest

    carry = (blank, stack_blank, acc_blank, acc_blank)
    carry = lax.fori_loop(0, ticks - 1, backward_step, carry)
    _, (grads_in, acc_down, acc_up) = backward_tick(ticks - 1, carry)
    grad_down, grad_up = side_by_side(
        (acc_down.astype(jnp.bfloat16), acc_up.astype(jnp.bfloat16)), "dp", 2, 0
    )
    return (outs[None, :, None], grads_in[None, :, None], grad_down[None], grad_up[None])


def solution(mesh):
    in_specs = (
        P(None, "dp", None, None),
        P("segment", "dp", None),
        P("segment", None),
        P("segment", None, None, None),
        P("segment", None, None, None),
        P(),
        P(),
        P(),
        P(None, "dp", None, None),
    )
    out_specs = (
        P("segment", None, "dp", None, None),
        P("segment", None, "dp", None, None),
        P("segment", None, None, "dp"),
        P("segment", None, None, "dp"),
    )
    return jax.shard_map(shards, mesh=mesh, in_specs=in_specs, out_specs=out_specs, check_vma=False)
```

profile of v0, /device:TPU:0, one launch (start us, length us, event | category | flops | bytes accessed | tf_op | source)
XLA Modules:
  0.0 870.6 jit_solution(13723919812734326416)
XLA Ops:
  16.4 193.5 %all-gather.3.cloned.1.call-done = bf16[1,4096,4096]{2,1,0:T(8,128)(2,1)} async-done(((bf16[1,256,4096]{2,1,0:T(8,128)(2,1)}), bf16[1,4096,4096]{2,1,0:T(8,128)(2,1)}) %all-gather.3.cloned.1.call-update) | async-done | bytes 33554448 | tf_op jit(solution)/shard_map/all_gather | solution.py:88
  212.8 230.3 %while.40 = (s32[]{:T(128)}, bf16[128,4096]{1,0:T(8,128)(2,1)}, bf16[2,128,4096]{2,1,0:T(8,128)(2,1)S(1)}, bf16[2,128,4096]{2,1,0:T(8,128)(2,1)}, s32[]{:T(128)}...) while((s32[]{:T(128)}, bf16[128,4096]{1,0:T(8,128)(2,1)}, ...), condition=%wide.region_5.6_spmd, body=%wide.region_1.5_spmd.sunk | while | flops 4321182720 | bytes 60985708 | solution.py:149
  214.7 23.2 %conditional.9 = (bf16[128,4096]{1,0:T(8,128)(2,1)}, bf16[1,128,4096]{2,1,0:T(8,128)(2,1)}) conditional(s32[]{:T(128)} %convert_element_type.345, () %tuple.153, (bf16[128,4096]{1,0:T(8,128)(2,1)S(1)}, f32[1,4096]{1,0:T(1,128)S(1)}, bf16[4096,4096]{1,0:T(8,128)(2,1)}, s32[]{:T(128)}, bf16[2,8,4096]{2,1,0:T(8,128)(2,1)S(1)}, ...), branch_computations={%region_2.2_spmd, %region_3.4_spmd} | conditional | flops 4319609856 | bytes 44207664 | solution.py:129
  215.0 16.5 %convolution_add_fusion.1 = f32[128,4096]{1,0:T(8,128)} fusion(bf16[4096,4096]{1,0:T(8,128)(2,1)} %get-tuple-element.684, bf16[128,4096]{1,0:T(8,128)(2,1)S(1)} %get-tuple-element.682, f32[4096]{0:T(1024)S(1)} %bitcast.186, f32[128]{0:T(128)S(1)} %add_rsqrt_fusion), kind=kOutput, calls=%fused_computation.1 | convolution fusion | flops 4298113024 | bytes 36717056 | tf_op jit(solution)/shard_map/while/body/eval_jaxpr/cond/branch_1_fun/dot_general | solution.py:45
  244.8 23.2 %conditional.9 = (bf16[128,4096]{1,0:T(8,128)(2,1)}, bf16[1,128,4096]{2,1,0:T(8,128)(2,1)}) conditional(s32[]{:T(128)} %convert_element_type.345, () %tuple.153, (bf16[128,4096]{1,0:T(8,128)(2,1)S(1)}, f32[1,4096]{1,0:T(1,128)S(1)}, bf16[4096,4096]{1,0:T(8,128)(2,1)}, s32[]{:T(128)}, bf16[2,8,4096]{2,1,0:T(8,128)(2,1)S(1)}, ...), branch_computations={%region_2.2_spmd, %region_3.4_spmd} | conditional | flops 4319609856 | bytes 44207664 | solution.py:129
  245.1 16.5 %convolution_add_fusion.1 = f32[128,4096]{1,0:T(8,128)} fusion(bf16[4096,4096]{1,0:T(8,128)(2,1)} %get-tuple-element.684, bf16[128,4096]{1,0:T(8,128)(2,1)S(1)} %get-tuple-element.682, f32[4096]{0:T(1024)S(1)} %bitcast.186, f32[128]{0:T(128)S(1)} %add_rsqrt_fusion), kind=kOutput, calls=%fused_computation.1 | convolution fusion | flops 4298113024 | bytes 36717056 | tf_op jit(solution)/shard_map/while/body/eval_jaxpr/cond/branch_1_fun/dot_general | solution.py:45
  278.1 32.4 %collective-permute-start = (bf16[128,4096]{1,0:T(8,128)(2,1)}, bf16[128,4096]{1,0:T(8,128)(2,1)S(1)}, u32[]{:S(2)}, u32[]{:S(2)}) collective-permute-start(bf16[128,4096]{1,0:T(8,128)(2,1)} %get-tuple-element.1159), channel_id=1, source_target_pairs={{0,16},{16,32},{32,48},{48,64},{64,80},{80,96},{96,112},{1,17},{17... | collective-permute-start | bytes 3145736 | tf_op jit(solution)/shard_map/while/body/eval_jaxpr/ppermute | solution.py:12
  318.0 14.1 %collective-permute-start = (bf16[128,4096]{1,0:T(8,128)(2,1)}, bf16[128,4096]{1,0:T(8,128)(2,1)S(1)}, u32[]{:S(2)}, u32[]{:S(2)}) collective-permute-start(bf16[128,4096]{1,0:T(8,128)(2,1)} %get-tuple-element.1159), channel_id=1, source_target_pairs={{0,16},{16,32},{32,48},{48,64},{64,80},{80,96},{96,112},{1,17},{17... | collective-permute-start | bytes 3145736 | tf_op jit(solution)/shard_map/while/body/eval_jaxpr/ppermute | solution.py:12
  339.6 35.1 %collective-permute-start = (bf16[128,4096]{1,0:T(8,128)(2,1)}, bf16[128,4096]{1,0:T(8,128)(2,1)S(1)}, u32[]{:S(2)}, u32[]{:S(2)}) collective-permute-start(bf16[128,4096]{1,0:T(8,128)(2,1)} %get-tuple-element.1159), channel_id=1, source_target_pairs={{0,16},{16,32},{32,48},{48,64},{64,80},{80,96},{96,112},{1,17},{17... | collective-permute-start | bytes 3145736 | tf_op jit(solution)/shard_map/while/body/eval_jaxpr/ppermute | solution.py:12
  382.3 14.1 %collective-permute-start = (bf16[128,4096]{1,0:T(8,128)(2,1)}, bf16[128,4096]{1,0:T(8,128)(2,1)S(1)}, u32[]{:S(2)}, u32[]{:S(2)}) collective-permute-start(bf16[128,4096]{1,0:T(8,128)(2,1)} %get-tuple-element.1159), channel_id=1, source_target_pairs={{0,16},{16,32},{32,48},{48,64},{64,80},{80,96},{96,112},{1,17},{17... | collective-permute-start | bytes 3145736 | tf_op jit(solution)/shard_map/while/body/eval_jaxpr/ppermute | solution.py:12
  403.9 14.1 %collective-permute-start = (bf16[128,4096]{1,0:T(8,128)(2,1)}, bf16[128,4096]{1,0:T(8,128)(2,1)S(1)}, u32[]{:S(2)}, u32[]{:S(2)}) collective-permute-start(bf16[128,4096]{1,0:T(8,128)(2,1)} %get-tuple-element.1159), channel_id=1, source_target_pairs={{0,16},{16,32},{32,48},{48,64},{64,80},{80,96},{96,112},{1,17},{17... | collective-permute-start | bytes 3145736 | tf_op jit(solution)/shard_map/while/body/eval_jaxpr/ppermute | solution.py:12
  425.5 14.1 %collective-permute-start = (bf16[128,4096]{1,0:T(8,128)(2,1)}, bf16[128,4096]{1,0:T(8,128)(2,1)S(1)}, u32[]{:S(2)}, u32[]{:S(2)}) collective-permute-start(bf16[128,4096]{1,0:T(8,128)(2,1)} %get-tuple-element.1159), channel_id=1, source_target_pairs={{0,16},{16,32},{32,48},{48,64},{64,80},{80,96},{96,112},{1,17},{17... | collective-permute-start | bytes 3145736 | tf_op jit(solution)/shard_map/while/body/eval_jaxpr/ppermute | solution.py:12
  448.6 355.2 %while.41 = (s32[]{:T(128)}, bf16[128,4096]{1,0:T(8,128)(2,1)}, bf16[2,128,4096]{2,1,0:T(8,128)(2,1)}, f32[16,8,4096]{2,1,0:T(8,128)}, f32[16,8,4096]{2,1,0:T(8,...) while((s32[]{:T(128)}, bf16[128,4096]{1,0:T(8,128)(2,1)}, ...), condition=%wide.region_14.15_spmd.clone, body=%wide.region_9.14_spmd.clone.sunk | while | flops 4354214400 | bytes 94118616 | solution.py:189
  458.2 25.3 %collective-permute-done.1 = bf16[128,4096]{1,0:T(8,128)(2,1)S(1)} collective-permute-done((bf16[128,4096]{1,0:T(8,128)(2,1)}, bf16[128,4096]{1,0:T(8,128)(2,1)S(1)}, u32[]{:S(2)}, u32[]{:S(2)}) %collective-permute-start.1) | collective-permute-done | bytes 1048608 | tf_op jit(solution)/shard_map/while/body/eval_jaxpr/ppermute | solution.py:12
  495.6 8.0 collective-permute-done.1
  535.5 7.9 collective-permute-done.1
  555.5 23.4 %collective-permute-done.1 = bf16[128,4096]{1,0:T(8,128)(2,1)S(1)} collective-permute-done((bf16[128,4096]{1,0:T(8,128)(2,1)}, bf16[128,4096]{1,0:T(8,128)(2,1)S(1)}, u32[]{:S(2)}, u32[]{:S(2)}) %collective-permute-start.1) | collective-permute-done | bytes 1048608 | tf_op jit(solution)/shard_map/while/body/eval_jaxpr/ppermute | solution.py:12
  591.1 8.0 collective-permute-done.1
  611.3 148.2 %collective-permute-done.1 = bf16[128,4096]{1,0:T(8,128)(2,1)S(1)} collective-permute-done((bf16[128,4096]{1,0:T(8,128)(2,1)}, bf16[128,4096]{1,0:T(8,128)(2,1)S(1)}, u32[]{:S(2)}, u32[]{:S(2)}) %collective-permute-start.1) | collective-permute-done | bytes 1048608 | tf_op jit(solution)/shard_map/while/body/eval_jaxpr/ppermute | solution.py:12
  760.5 25.9 %conditional.10 = (bf16[128,4096]{1,0:T(8,128)(2,1)}, f32[8,4096]{1,0:T(8,128)S(1)}, f32[8,4096]{1,0:T(8,128)S(1)}, bf16[1,128,4096]{2,1,0:T(8,128)(2,1)}) conditional(s32[]{:T(128)} %convert_element_type.346, () %tuple.157, (pred[]{:T(512)}, bf16[2,128,4096]{2,1,0:T(8,128)(2,1)}, s32[]{:T(128)}, bf16[128,4096]{1,0:T(8,128)(2,1)}, ...), branch_computations={%region_10.10_spmd, %region_11.13_spmd} | conditional | flops 4350544384 | bytes 57155172 | solution.py:168
  763.4 16.0 %fusion.153 = f32[128,4096]{1,0:T(8,128)S(1)} fusion(bf16[128,4096]{1,0:T(8,128)(2,1)S(1)} %bitcast_select_fusion.2, bf16[4096,4096]{1,0:T(8,128)(2,1)} %get-tuple-element.714), kind=kOutput, calls=%fused_computation.169 | convolution fusion | flops 4294967296 | bytes 36700160 | tf_op jit(solution)/shard_map/while/body/eval_jaxpr/cond/branch_1_fun/dot_general | solution.py:52
  803.8 23.6 %conditional.5 = (f32[8,4096]{1,0:T(8,128)}, f32[8,4096]{1,0:T(8,128)}, bf16[1,128,4096]{2,1,0:T(8,128)(2,1)}) conditional(s32[]{:T(128)} %convert_element_type.171, () %tuple.98, (pred[]{:T(512)}, bf16[2,128,4096]{2,1,0:T(8,128)(2,1)}, s32[]{:T(128)}, bf16[128,4096]{1,0:T(8,128)(2,1)}, bf16[2,8,4096]{2,0,1:T(2,128)(2,1)}, ...), branch_computations={%region_15.16_spmd, %region_16.19_spmd} | conditional | flops 4350544384 | bytes 56620128 | solution.py:168
  805.9 16.0 %fusion.154 = f32[128,4096]{1,0:T(8,128)S(1)} fusion(bf16[128,4096]{1,0:T(8,128)(2,1)S(1)} %bitcast_select_fusion.3, bf16[4096,4096]{1,0:T(8,128)(2,1)} %get-tuple-element.744), kind=kOutput, calls=%fused_computation.170 | convolution fusion | flops 4294967296 | bytes 36700160 | tf_op jit(solution)/shard_map/cond/branch_1_fun/dot_general | solution.py:52
  847.8 13.3 %all-to-all-done = bf16[16,32,8,256]{3,2,1,0:T(8,128)(2,1)} async-done(((bf16[16,32,8,256]{3,2,1,0:T(8,128)(2,1)}), bf16[16,32,8,256]{3,2,1,0:T(8,128)(2,1)}, u32[]{:S(2)}, u32[]{:S(2)}) %all-to-all-start) | async-done | bytes 2097184 | tf_op jit(solution)/shard_map/all_to_all | solution.py:22
  (274 shorter events, 269.1 us)
Async XLA Ops:
  7.2 202.7 %all-gather.3.cloned.1.call-start = ((), (), s32[]{:S(2)}) async-start(), calls=%async_computation.1 | async-start | bytes 35651584 | tf_op jit(solution)/shard_map/all_gather | solution.py:88
  237.8 4.1 collective-permute-start
  268.0 5.1 collective-permute-start
  278.1 34.9 %collective-permute-start = (bf16[128,4096]{1,0:T(8,128)(2,1)}, bf16[128,4096]{1,0:T(8,128)(2,1)S(1)}, u32[]{:S(2)}, u32[]{:S(2)}) collective-permute-start(bf16[128,4096]{1,0:T(8,128)(2,1)} %get-tuple-element.1159), channel_id=1, source_target_pairs={{0,16},{16,32},{32,48},{48,64},{64,80},{80,96},{96,112},{1,17},{17... | collective-permute-start | bytes 3145736 | tf_op jit(solution)/shard_map/while/body/eval_jaxpr/ppermute | solution.py:12
  318.0 16.6 %collective-permute-start = (bf16[128,4096]{1,0:T(8,128)(2,1)}, bf16[128,4096]{1,0:T(8,128)(2,1)S(1)}, u32[]{:S(2)}, u32[]{:S(2)}) collective-permute-start(bf16[128,4096]{1,0:T(8,128)(2,1)} %get-tuple-element.1159), channel_id=1, source_target_pairs={{0,16},{16,32},{32,48},{48,64},{64,80},{80,96},{96,112},{1,17},{17... | collective-permute-start | bytes 3145736 | tf_op jit(solution)/shard_map/while/body/eval_jaxpr/ppermute | solution.py:12
  339.6 37.6 %collective-permute-start = (bf16[128,4096]{1,0:T(8,128)(2,1)}, bf16[128,4096]{1,0:T(8,128)(2,1)S(1)}, u32[]{:S(2)}, u32[]{:S(2)}) collective-permute-start(bf16[128,4096]{1,0:T(8,128)(2,1)} %get-tuple-element.1159), channel_id=1, source_target_pairs={{0,16},{16,32},{32,48},{48,64},{64,80},{80,96},{96,112},{1,17},{17... | collective-permute-start | bytes 3145736 | tf_op jit(solution)/shard_map/while/body/eval_jaxpr/ppermute | solution.py:12
  382.3 16.6 %collective-permute-start = (bf16[128,4096]{1,0:T(8,128)(2,1)}, bf16[128,4096]{1,0:T(8,128)(2,1)S(1)}, u32[]{:S(2)}, u32[]{:S(2)}) collective-permute-start(bf16[128,4096]{1,0:T(8,128)(2,1)} %get-tuple-element.1159), channel_id=1, source_target_pairs={{0,16},{16,32},{32,48},{48,64},{64,80},{80,96},{96,112},{1,17},{17... | collective-permute-start | bytes 3145736 | tf_op jit(solution)/shard_map/while/body/eval_jaxpr/ppermute | solution.py:12
  403.9 16.6 %collective-permute-start = (bf16[128,4096]{1,0:T(8,128)(2,1)}, bf16[128,4096]{1,0:T(8,128)(2,1)S(1)}, u32[]{:S(2)}, u32[]{:S(2)}) collective-permute-start(bf16[128,4096]{1,0:T(8,128)(2,1)} %get-tuple-element.1159), channel_id=1, source_target_pairs={{0,16},{16,32},{32,48},{48,64},{64,80},{80,96},{96,112},{1,17},{17... | collective-permute-start | bytes 3145736 | tf_op jit(solution)/shard_map/while/body/eval_jaxpr/ppermute | solution.py:12
  425.5 16.6 %collective-permute-start = (bf16[128,4096]{1,0:T(8,128)(2,1)}, bf16[128,4096]{1,0:T(8,128)(2,1)S(1)}, u32[]{:S(2)}, u32[]{:S(2)}) collective-permute-start(bf16[128,4096]{1,0:T(8,128)(2,1)} %get-tuple-element.1159), channel_id=1, source_target_pairs={{0,16},{16,32},{32,48},{48,64},{64,80},{80,96},{96,112},{1,17},{17... | collective-permute-start | bytes 3145736 | tf_op jit(solution)/shard_map/while/body/eval_jaxpr/ppermute | solution.py:12
  450.8 32.6 %collective-permute-start.1 = (bf16[128,4096]{1,0:T(8,128)(2,1)}, bf16[128,4096]{1,0:T(8,128)(2,1)S(1)}, u32[]{:S(2)}, u32[]{:S(2)}) collective-permute-start(bf16[128,4096]{1,0:T(8,128)(2,1)} %get-tuple-element.1176), channel_id=1, source_target_pairs={{16,0},{32,16},{48,32},{64,48},{80,64},{96,80},{112,96},{17,1},{33... | collective-permute-start | bytes 3145736 | tf_op jit(solution)/shard_map/while/body/eval_jaxpr/ppermute | solution.py:12
  458.2 25.3 %copy-start.3 = (f32[16,8,4096]{2,1,0:T(8,128)}, f32[16,8,4096]{2,1,0:T(8,128)S(1)}, u32[]{:S(2)}) copy-start(f32[16,8,4096]{2,1,0:T(8,128)S(1)} %get-tuple-element.1273) | copy-start | bytes 6291460 | tf_op jit(solution)/shard_map/while
  486.7 17.0 %collective-permute-start.1 = (bf16[128,4096]{1,0:T(8,128)(2,1)}, bf16[128,4096]{1,0:T(8,128)(2,1)S(1)}, u32[]{:S(2)}, u32[]{:S(2)}) collective-permute-start(bf16[128,4096]{1,0:T(8,128)(2,1)} %get-tuple-element.1176), channel_id=1, source_target_pairs={{16,0},{32,16},{48,32},{64,48},{80,64},{96,80},{112,96},{17,1},{33... | collective-permute-start | bytes 3145736 | tf_op jit(solution)/shard_map/while/body/eval_jaxpr/ppermute | solution.py:12
  506.9 16.3 %collective-permute-start.1 = (bf16[128,4096]{1,0:T(8,128)(2,1)}, bf16[128,4096]{1,0:T(8,128)(2,1)S(1)}, u32[]{:S(2)}, u32[]{:S(2)}) collective-permute-start(bf16[128,4096]{1,0:T(8,128)(2,1)} %get-tuple-element.1176), channel_id=1, source_target_pairs={{16,0},{32,16},{48,32},{64,48},{80,64},{96,80},{112,96},{17,1},{33... | collective-permute-start | bytes 3145736 | tf_op jit(solution)/shard_map/while/body/eval_jaxpr/ppermute | solution.py:12
  526.5 16.8 %collective-permute-start.1 = (bf16[128,4096]{1,0:T(8,128)(2,1)}, bf16[128,4096]{1,0:T(8,128)(2,1)S(1)}, u32[]{:S(2)}, u32[]{:S(2)}) collective-permute-start(bf16[128,4096]{1,0:T(8,128)(2,1)} %get-tuple-element.1176), channel_id=1, source_target_pairs={{16,0},{32,16},{48,32},{64,48},{80,64},{96,80},{112,96},{17,1},{33... | collective-permute-start | bytes 3145736 | tf_op jit(solution)/shard_map/while/body/eval_jaxpr/ppermute | solution.py:12
  546.6 32.3 %collective-permute-start.1 = (bf16[128,4096]{1,0:T(8,128)(2,1)}, bf16[128,4096]{1,0:T(8,128)(2,1)S(1)}, u32[]{:S(2)}, u32[]{:S(2)}) collective-permute-start(bf16[128,4096]{1,0:T(8,128)(2,1)} %get-tuple-element.1176), channel_id=1, source_target_pairs={{16,0},{32,16},{48,32},{64,48},{80,64},{96,80},{112,96},{17,1},{33... | collective-permute-start | bytes 3145736 | tf_op jit(solution)/shard_map/while/body/eval_jaxpr/ppermute | solution.py:12
  555.5 23.4 %copy-start.3 = (f32[16,8,4096]{2,1,0:T(8,128)}, f32[16,8,4096]{2,1,0:T(8,128)S(1)}, u32[]{:S(2)}) copy-start(f32[16,8,4096]{2,1,0:T(8,128)S(1)} %get-tuple-element.1273) | copy-start | bytes 6291460 | tf_op jit(solution)/shard_map/while
  582.2 17.0 %collective-permute-start.1 = (bf16[128,4096]{1,0:T(8,128)(2,1)}, bf16[128,4096]{1,0:T(8,128)(2,1)S(1)}, u32[]{:S(2)}, u32[]{:S(2)}) collective-permute-start(bf16[128,4096]{1,0:T(8,128)(2,1)} %get-tuple-element.1176), channel_id=1, source_target_pairs={{16,0},{32,16},{48,32},{64,48},{80,64},{96,80},{112,96},{17,1},{33... | collective-permute-start | bytes 3145736 | tf_op jit(solution)/shard_map/while/body/eval_jaxpr/ppermute | solution.py:12
  602.4 157.1 %collective-permute-start.1 = (bf16[128,4096]{1,0:T(8,128)(2,1)}, bf16[128,4096]{1,0:T(8,128)(2,1)S(1)}, u32[]{:S(2)}, u32[]{:S(2)}) collective-permute-start(bf16[128,4096]{1,0:T(8,128)(2,1)} %get-tuple-element.1176), channel_id=1, source_target_pairs={{16,0},{32,16},{48,32},{64,48},{80,64},{96,80},{112,96},{17,1},{33... | collective-permute-start | bytes 3145736 | tf_op jit(solution)/shard_map/while/body/eval_jaxpr/ppermute | solution.py:12
  611.3 148.2 %copy-start.3 = (f32[16,8,4096]{2,1,0:T(8,128)}, f32[16,8,4096]{2,1,0:T(8,128)S(1)}, u32[]{:S(2)}) copy-start(f32[16,8,4096]{2,1,0:T(8,128)S(1)} %get-tuple-element.1273) | copy-start | bytes 6291460 | tf_op jit(solution)/shard_map/while
  763.4 16.0 %copy-start.17 = (bf16[128,8]{0,1:T(8,128)(2,1)}, bf16[128,8]{0,1:T(8,128)(2,1)S(1)}, u32[]{:S(2)}) copy-start(bf16[128,8]{0,1:T(8,128)(2,1)S(1)} %convolution_convert_fusion.1) | copy-start | bytes 6148 | tf_op jit(solution)/shard_map/while/body/eval_jaxpr/cond
  786.5 16.3 %collective-permute-start.1 = (bf16[128,4096]{1,0:T(8,128)(2,1)}, bf16[128,4096]{1,0:T(8,128)(2,1)S(1)}, u32[]{:S(2)}, u32[]{:S(2)}) collective-permute-start(bf16[128,4096]{1,0:T(8,128)(2,1)} %get-tuple-element.1176), channel_id=1, source_target_pairs={{16,0},{32,16},{48,32},{64,48},{80,64},{96,80},{112,96},{17,1},{33... | collective-permute-start | bytes 3145736 | tf_op jit(solution)/shard_map/while/body/eval_jaxpr/ppermute | solution.py:12
  805.9 16.0 %copy-start.12 = (bf16[2,8,4096]{2,0,1:T(2,128)(2,1)S(1)}, bf16[2,8,4096]{2,0,1:T(2,128)(2,1)}, u32[]{:S(2)}) copy-start(bf16[2,8,4096]{2,0,1:T(2,128)(2,1)} %get-tuple-element.936) | copy-start | bytes 393220 | tf_op jit(solution)/shard_map/cond
  833.1 28.0 %all-to-all-start = ((bf16[16,32,8,256]{3,2,1,0:T(8,128)(2,1)}), bf16[16,32,8,256]{3,2,1,0:T(8,128)(2,1)}, u32[]{:S(2)}, u32[]{:S(2)}) async-start(bf16[16,32,8,256]{3,2,1,0:T(8,128)(2,1)} %copy.43), calls=%async_computation | async-start | bytes 4194304 | tf_op jit(solution)/shard_map/all_to_all | solution.py:22
  843.7 20.0 %copy-start.1 = (bf16[1,16,8,4096]{3,2,1,0:T(8,128)(2,1)S(1)}, bf16[1,16,8,4096]{3,2,1,0:T(8,128)(2,1)}, u32[]{:S(2)}) copy-start(bf16[1,16,8,4096]{3,2,1,0:T(8,128)(2,1)} %param.24) | copy-start | bytes 3145732
  (45 other events, 134.7 us)
Sparse Core Ops, SparseCore 0:
  10.2 199.6 all-gather.2
where the time goes:
time: 873 us; the launch traced here: 871 us
  waiting for transfers between devices  443 us (51%)
  starting transfers between devices  143 us (16%)
  other arithmetic  111 us (13%)
  matrix products  84.4 us (10%)
  local copies, waits for them, and re-layouts  74.1 us (8%)
  between operations  14.3 us (2%)
    ppermute x16, waiting for transfers between devices, shifted(): return lax.ppermute(block, axis, route)  235 us
    all_gather x1, waiting for transfers between devices, shards(): weight = lax.all_gather(base_weight[0], 'dp', axis=0, tiled=True)  194 us
    ppermute x16, starting transfers between devices, shifted(): return lax.ppermute(block, axis, route)  138 us
    select_n x26, other arithmetic, place(): jnp.where(active, lax.dynamic_update_index_in_dim(table, value, index, 0)...  62.3 us
    dot_general x2, matrix products, forward_full(): jnp.dot(normed, weight, preferred_element_type=jnp.float32)  33 us
    add x8, other arithmetic, backward_tick(): acc_up = acc_up + weights * seq_up[None]  32.8 us
    dot_general x2, matrix products, backward_core(): dnorm = jnp.dot(grad_out, weight.T, preferred_element_type=jnp.float32)  32 us
  transfers between devices with their start and end apart: 18, of which 10 were waited for; matrix products, arithmetic and copies ran while one was open for 11% of the time, Pallas kernels for 0%

commit v1 on v0

v1 whole, which is shorter than its diff:
```python
import functools

import jax
import jax.numpy as jnp
from jax import lax
from jax.experimental import pallas as pl
from jax.experimental.pallas import tpu as pltpu
from jax.sharding import PartitionSpec as P

EPS = 1e-06
MESH = pl.DeviceIdType.MESH
SIDE = 4
CHUNKS = 4
F32 = jnp.float32
BF16 = jnp.bfloat16


def dot(a, b, dims=((1,), (0,))):
    return lax.dot_general(a, b, (dims, ((), ())), preferred_element_type=F32)


def kernel(
    emb, w, gain, sdown, sup, tasks, alloc, lens, cot,
    hidden, grads_in, gdown, gup,
    wbuf, xbuf, obuf, hbuf, gbuf, gout, down, up, lowbuf, invbuf, mixb, mixrow, seq, got,
    first_s, first_r, second_s, second_r, own_sem,
    x_s, x_r, g_s, g_r, load_sem, store_sem, seq_s, seq_r,
):
    segments = lax.axis_size("segment")
    members = lax.axis_size("dp")
    seg = lax.axis_index("segment")
    me = lax.axis_index("dp")
    micro, rows, width = emb.shape
    block = w.shape[0]
    half = width // 2
    part = block // 2
    skills, rank = sdown.shape[0], sdown.shape[1]
    z, y = me // SIDE, lax.rem(me, SIDE)
    last = segments - 1

    barrier = pltpu.get_barrier_semaphore()

    def greet(d, c):
        pl.semaphore_signal(barrier, inc=1, device_id=(seg, lax.rem(me + d, members)), device_id_type=MESH)
        return c

    lax.fori_loop(1, members, greet, 0)
    for d in (1, segments - 1):
        pl.semaphore_signal(barrier, inc=1, device_id=(lax.rem(seg + d, segments), me), device_id_type=MESH)
    pl.semaphore_wait(barrier, members + 1)

    def at(h, df, ds):
        dy, dz = (df, ds) if h == 0 else (ds, df)
        return lax.rem(z + dz + SIDE, SIDE) * SIDE + lax.rem(y + dy + SIDE, SIDE)

    def rows_of(h, df, ds, sub=None):
        start = at(h, df, ds) * block
        if sub is None:
            return wbuf.at[h, pl.ds(pl.multiple_of(start, block), block), :]
        return wbuf.at[h, pl.ds(pl.multiple_of(start + sub * part, part), part), :]

    def send(src, dst, s, r, to):
        c = pltpu.make_async_remote_copy(
            src_ref=src, dst_ref=dst, send_sem=s, recv_sem=r, device_id=(seg, to), device_id_type=MESH
        )
        c.start()
        return c

    sent = []
    first = [[None] * 4 for _ in range(2)]
    second = [[[None] * 4 for _ in range(4)] for _ in range(2)]
    order = (0, -1, 1, 2)
    own = []
    for h in range(2):
        mine = w.at[:, h * half : (h + 1) * half]
        for d, way in enumerate((1, -1)):
            first[h][d] = send(mine, rows_of(h, 0, 0), first_s.at[h, d], first_r.at[h, d], at(h, way, 0))
    for h in range(2):
        mine = w.at[:, h * half : (h + 1) * half]
        for d, way in enumerate((1, -1)):
            second[h][0][d] = send(mine, rows_of(h, 0, 0), second_s.at[h, 0, d], second_r.at[h, 0, d], at(h, 0, way))
    for h in range(2):
        c = pltpu.make_async_copy(w.at[:, h * half : (h + 1) * half], rows_of(h, 0, 0), own_sem.at[h])
        c.start()
        own.append(c)

    @pl.when(seg == 0)
    def _():
        pltpu.make_async_copy(emb, xbuf, load_sem.at[0]).start()

    @pl.when(seg == last)
    def _():
        pltpu.make_async_copy(cot, gbuf, load_sem.at[1]).start()

    table = alloc[...].astype(F32).astype(BF16)
    total = alloc.shape[0]
    picked = (tasks[...] == lax.broadcasted_iota(jnp.int32, (tasks.shape[0], total), 1)).astype(F32).astype(BF16)
    uses = dot(picked, table)
    mix = uses / jnp.maximum(jnp.sum(uses, axis=1, keepdims=True), 1.0)
    for s in range(skills):
        mixb[s] = jnp.broadcast_to(mix[:, s : s + 1], mixb.shape[1:])
    step = mixb.shape[2]

    def adapters(i, c):
        cols = pl.ds(pl.multiple_of(i * step, step), step)
        for m in range(micro):
            for source, target in ((sdown, down), (sup, up)):
                acc = jnp.zeros((rank, step), F32)
                for s in range(skills):
                    acc = acc + mixb[s, pl.ds(m * members + me, 1), :] * source[s, :, cols].astype(F32)
                target[m, :, cols] = acc.astype(BF16)
        return c

    lax.fori_loop(0, width // step, adapters, 0)

    def arrived_first(h):
        for d, way in enumerate((1, -1)):
            first[h][d].wait_recv()
            src = rows_of(h, -way, 0, d)
            first[h][2 + d] = send(src, src, first_s.at[h, 2 + d], first_r.at[h, 2 + d], at(h, way, 0))

    def spread(h, i):
        for d, way in enumerate((1, -1)):
            src = rows_of(h, order[i], 0)
            second[h][i][d] = send(src, src, second_s.at[h, i, d], second_r.at[h, i, d], at(h, 0, way))

    def pass_on(h, i):
        for d, way in enumerate((1, -1)):
            second[h][i][d].wait_recv()
            src = rows_of(h, order[i], -way, d)
            second[h][i][2 + d] = send(src, src, second_s.at[h, i, 2 + d], second_r.at[h, i, 2 + d], at(h, 0, way))

    for h in range(2):
        arrived_first(h)
    for h in range(2):
        spread(h, 1)
        spread(h, 2)
    for h in range(2):
        pass_on(h, 0)
    for h in range(2):
        first[h][2].wait_recv()
        first[h][3].wait_recv()
        spread(h, 3)
    for i in (1, 2, 3):
        for h in range(2):
            pass_on(h, i)
    for h in range(2):
        own[h].wait()
        for i in range(4):
            second[h][i][2].wait_recv()
            second[h][i][3].wait_recv()
    for h in range(2):
        for d in range(4):
            first[h][d].wait_send()
            for i in range(4):
                second[h][i][d].wait_send()

    wide = width // CHUNKS
    tile = 512

    def hop(buf, target, m, q, s, r, to):
        cols = pl.ds(q * wide, wide)
        return pltpu.make_async_remote_copy(
            src_ref=buf.at[m, :, cols], dst_ref=target.at[m, :, cols], send_sem=s.at[m, q], recv_sem=r.at[m, q],
            device_id=(to, me), device_id_type=MESH,
        )

    onward = functools.partial(hop, obuf, xbuf, s=x_s, r=x_r, to=lax.rem(seg + 1, segments))
    back = functools.partial(hop, gout, gbuf, s=g_s, r=g_r, to=lax.rem(seg + last, segments))

    @pl.when(seg == 0)
    def _():
        pltpu.make_async_copy(emb, xbuf, load_sem.at[0]).wait()

    for m in range(micro):

        @pl.when(seg > 0)
        def _():
            for q in range(CHUNKS):
                onward(m, q).wait_recv()

        def squares(i, acc):
            v = xbuf[m, :, pl.ds(pl.multiple_of(i * tile, tile), tile)].astype(F32)
            return acc + jnp.sum(v * v, axis=1, keepdims=True)

        ss = lax.fori_loop(0, width // tile, squares, jnp.zeros((rows, 1), F32))
        inv = lax.rsqrt(ss / width + EPS)
        invbuf[m] = inv

        def normed(i, c):
            cols = pl.ds(pl.multiple_of(i * tile, tile), tile)
            hbuf[m, :, cols] = (xbuf[m, :, cols].astype(F32) * inv * gain[:, cols]).astype(BF16)
            return c

        lax.fori_loop(0, width // tile, normed, 0)
        low = dot(hbuf[m], down[m], ((1,), (1,))).astype(BF16)
        lowbuf[m] = low
        for q in range(CHUNKS):

            def forward(i, c):
                at_col = q * wide + i * tile
                cols = pl.ds(pl.multiple_of(at_col, tile), tile)
                inner = pl.ds(pl.multiple_of(at_col - (q * wide // half) * half, tile), tile)
                acc = dot(hbuf[m], wbuf[q * wide // half, :, inner])
                acc = acc + dot(low, up[m, :, cols])
                obuf[m, :, cols] = (xbuf[m, :, cols].astype(F32) + acc).astype(BF16)
                return c

            lax.fori_loop(0, wide // tile, forward, 0)

            @pl.when(seg < last)
            def _():
                onward(m, q).start()

        pltpu.make_async_copy(obuf.at[m], hidden.at[m], store_sem.at[m]).start()

    @pl.when(seg == last)
    def _():
        pltpu.make_async_copy(cot, gbuf, load_sem.at[1]).wait()
        for m in range(micro):
            keep = lax.broadcasted_iota(jnp.int32, (rows, tile), 0) < lens[m, me]

            def masked(i, c):
                cols = pl.ds(pl.multiple_of(i * tile, tile), tile)
                gbuf[m, :, cols] = jnp.where(keep, gbuf[m, :, cols].astype(F32), 0.0).astype(BF16)
                return c

            lax.fori_loop(0, width // tile, masked, 0)

    btile = 256
    for m in range(micro):

        @pl.when(seg < last)
        def _():
            for q in range(CHUNKS):
                back(m, q).wait_recv()

        glow = dot(gbuf[m], up[m], ((1,), (1,))).astype(BF16)
        inv = invbuf[m]

        def along(i, acc):
            cols = pl.ds(pl.multiple_of(i * tile, tile), tile)
            step_out = obuf[m, :, cols].astype(F32) - xbuf[m, :, cols].astype(F32)
            return acc + jnp.sum(gbuf[m, :, cols].astype(F32) * step_out, axis=1, keepdims=True)

        coef = lax.fori_loop(0, width // tile, along, jnp.zeros((rows, 1), F32)) / width * inv * inv
        for q in range(CHUNKS):

            def backward(i, c):
                cols = pl.ds(pl.multiple_of(q * wide + i * btile, btile), btile)
                dh = dot(gbuf[m, :, :half], wbuf[0, cols, :], ((1,), (1,)))
                dh = dh + dot(gbuf[m, :, half:], wbuf[1, cols, :], ((1,), (1,)))
                dh = dh + dot(glow, down[m, :, cols])
                out = gbuf[m, :, cols].astype(F32) + inv * (gain[:, cols] * dh) - xbuf[m, :, cols].astype(F32) * coef
                gout[m, :, cols] = out.astype(BF16)
                return c

            lax.fori_loop(0, wide // btile, backward, 0)

            @pl.when(seg > 0)
            def _():
                back(m, q).start()

        pltpu.make_async_copy(gout.at[m], grads_in.at[m], store_sem.at[micro + m]).start()

        def adapter_grads(i, c):
            cols = pl.ds(pl.multiple_of(i * tile, tile), tile)
            seq[m, :, cols] = dot(glow, hbuf[m, :, cols], ((0,), (0,)))
            seq[micro + m, :, cols] = dot(lowbuf[m], gbuf[m, :, cols], ((0,), (0,)))
            return c

        lax.fori_loop(0, width // tile, adapter_grads, 0)

    def share(d):
        to = lax.rem(me + d, members)
        return pltpu.make_async_remote_copy(
            src_ref=seq.at[:, :, pl.ds(pl.multiple_of(to * block, block), block)], dst_ref=got.at[d],
            send_sem=seq_s.at[d], recv_sem=seq_r.at[d], device_id=(seg, to), device_id_type=MESH,
        )

    def share_start(d, c):
        share(d).start()
        return c

    def add(mine, source, fresh):
        for t, target in enumerate((gdown, gup)):
            for s in range(skills):
                p = sum(mixb[s, pl.ds(m * members + source, 1), :] * mine[t * micro + m] for m in range(micro))
                p = p.astype(BF16).astype(F32)
                target[s] = p if fresh else target[s] + p

    lax.fori_loop(1, members, share_start, 0)
    own_cols = pl.ds(pl.multiple_of(me * block, block), block)
    add([seq[i, :, own_cols] for i in range(2 * micro)], me, True)

    def take(d, c):
        share(d).wait_recv()
        add([got[d, i] for i in range(2 * micro)], lax.rem(me - d + members, members), False)
        return c

    lax.fori_loop(1, members, take, 0)

    def drain(d, c):
        share(d).wait_send()
        return c

    lax.fori_loop(1, members, drain, 0)
    for m in range(micro):
        pltpu.make_async_copy(obuf.at[m], hidden.at[m], store_sem.at[m]).wait()
        pltpu.make_async_copy(gout.at[m], grads_in.at[m], store_sem.at[micro + m]).wait()

    @pl.when(seg < last)
    def _():
        for m in range(micro):
            for q in range(CHUNKS):
                onward(m, q).wait_send()

    @pl.when(seg > 0)
    def _():
        for m in range(micro):
            for q in range(CHUNKS):
                back(m, q).wait_send()


def shards(embeds, base_weight, norm_gain, skill_down, skill_up, task_ids, allocation, target_lengths, cotangent):
    micro, _, rows, width = embeds.shape
    block = base_weight.shape[1]
    _, skills, rank, _ = skill_down.shape
    members = lax.axis_size("dp")
    anywhere = pl.BlockSpec(memory_space=pl.ANY)
    vmem = pl.BlockSpec(memory_space=pltpu.VMEM)
    smem = pl.BlockSpec(memory_space=pltpu.SMEM)
    stream = jax.ShapeDtypeStruct((micro, rows, width), BF16)
    grad = jax.ShapeDtypeStruct((skills, rank, block), F32)
    dma = pltpu.SemaphoreType.DMA
    held = pltpu.VMEM((micro, rows, width), BF16)
    hidden, grads_in, gdown, gup = pl.pallas_call(
        kernel,
        out_shape=(stream, stream, grad, grad),
        in_specs=[anywhere, anywhere, vmem, vmem, vmem, vmem, vmem, smem, anywhere],
        out_specs=(anywhere, anywhere, vmem, vmem),
        scratch_shapes=[
            pltpu.VMEM((2, width, width // 2), BF16),
            held, held, held, held, held,
            pltpu.VMEM((micro, rank, width), BF16),
            pltpu.VMEM((micro, rank, width), BF16),
            pltpu.VMEM((micro, rows, rank), BF16),
            pltpu.VMEM((micro, rows, 1), F32),
            pltpu.VMEM((skills, micro * members, block), F32),
            pltpu.VMEM((8, 128), F32),
            pltpu.VMEM((2 * micro, rank, width), F32),
            pltpu.VMEM((members, 2 * micro, rank, block), F32),
            dma((2, 4)), dma((2, 4)), dma((2, 4, 4)), dma((2, 4, 4)), dma((2,)),
            dma((micro, CHUNKS)), dma((micro, CHUNKS)), dma((micro, CHUNKS)), dma((micro, CHUNKS)),
            dma((2,)), dma((2 * micro,)), dma((members,)), dma((members,)),
        ],
        compiler_params=pltpu.CompilerParams(
            collective_id=0, has_side_effects=True, vmem_limit_bytes=60 * 1024 * 1024
        ),
    )(
        embeds[:, 0], base_weight[0], norm_gain, skill_down[0], skill_up[0],
        task_ids.reshape(-1, 1), allocation, target_lengths, cotangent[:, 0],
    )
    return (hidden[None, :, None], grads_in[None, :, None], gdown[None], gup[None])


def solution(mesh):
    in_specs = (
        P(None, "dp", None, None),
        P("segment", "dp", None),
        P("segment", None),
        P("segment", None, None, None),
        P("segment", None, None, None),
        P(),
        P(),
        P(),
        P(None, "dp", None, None),
    )
    out_specs = (
        P("segment", None, "dp", None, None),
        P("segment", None, "dp", None, None),
        P("segment", None, None, "dp"),
        P("segment", None, None, "dp"),
    )
    return jax.shard_map(shards, mesh=mesh, in_specs=in_specs, out_specs=out_specs, check_vma=False)
```

time: 873 us -> 462 us (0.53)
  Pallas kernels: 0 us -> 452 us
  waiting for transfers between devices: 443 us -> 0 us
  starting transfers between devices: 143 us -> 0 us
  other arithmetic: 111 us -> 0 us
  matrix products: 84.4 us -> 0 us
  local copies, waits for them, and re-layouts: 74.1 us -> 9.44 us
  between operations: 14.3 us -> 0.65 us
    pallas_call x0 -> x1, Pallas kernels: none -> 452 us  [shards(): pl.pallas_call(kernel, out_shape=(stream, stream, grad, grad), in_specs=[...]
    ppermute x16 -> x0, waiting for transfers between devices: 235 us -> none  [shifted(): return lax.ppermute(block, axis, route)]
    all_gather x1 -> x0, waiting for transfers between devices: 194 us -> none  [shards(): weight = lax.all_gather(base_weight[0], 'dp', axis=0, tiled=True)]
    ppermute x16 -> x0, starting transfers between devices: 138 us -> none  [shifted(): return lax.ppermute(block, axis, route)]
    dot_general x17 -> x0, matrix products: 84.4 us -> none  [the longest x2 33 us: forward_full(): jnp.dot(normed, weight, preferred_element_type=jnp.float32)]
    select_n x28 -> x0, other arithmetic: 65.6 us -> none  [the longest x26 62.3 us: place(): jnp.where(active, lax.dynamic_update_index_in_dim(table, value, index, 0)...]
    broadcast_in_dim x33 -> x0, local copies, waits for them, and re-layouts: 36 us -> none  [the longest x15 16.7 us: shards(): blank = jnp.zeros((block_rows, width), jnp.bfloat16)]
    add x8 -> x0, other arithmetic: 32.8 us -> none  [backward_tick(): acc_up = acc_up + weights * seq_up[None]]
  transfers between devices with their start and end apart: 18 -> 0, of which waited for: 10 -> 0; matrix products, arithmetic and copies ran while one was open for 11% -> 0% of each run, Pallas kernels for 0% -> 0%
where the time goes in v1:
time: 462 us
  Pallas kernels  452 us (98%)
  local copies, waits for them, and re-layouts  9.44 us (2%)
    pallas_call x1, Pallas kernels, shards(): pl.pallas_call(kernel, out_shape=(stream, stream, grad, grad), in_specs=[...  452 us

profile of v1, /device:TPU:0, one launch (start us, length us, event | category | flops | bytes accessed | tf_op | source)
XLA Modules:
  0.0 461.8 jit_solution(8180121549405391049)
XLA Ops:
  0.6 1.4 reshape.12.tasks
  2.0 2.2 copy.14.alloc
  4.2 451.7 %shard_map.120 = (bf16[2,128,4096]{2,1,0:T(8,128)(2,1)}, bf16[2,128,4096]{2,1,0:T(8,128)(2,1)}, f32[16,8,256]{2,1,0:T(8,128)}, f32[16,8,256]{2,1,0:T(8,128)}) custom-call(bf16[2,128,4096]{2,1,0:T(8,128)(2,1)} %bitcast.15, bf16[256,4096]{1,0:T(8,128)(2,1)} %bitcast.16, f32[1,4096]{1,0:T(1,128)} %gain.1, bf16[16,8,4096]{2,1,0:T(8,128)(2,1)} %bitcast.18, ...), custom_call_target="tpu_custom_call" | custom-call | tf_op jit(solution)/shard_map/pallas_call | solution.py:337
  455.8 0.0 copy-start
  455.8 3.3 copy.21
  459.1 0.0 copy-done
  459.1 0.0 copy-start.2
  459.1 0.0 copy-start.1
  459.1 1.3 copy.22
  460.4 0.0 copy-done.2
  460.4 0.7 copy.23
  461.1 0.0 copy-done.1
  461.1 0.7 copy.24
Async XLA Ops:
  455.8 3.3 copy-start
  459.1 1.3 copy-start.2
  459.1 2.0 copy-start.1

commit v2 on v1

--- a/solution.py
+++ b/solution.py
@@ -22,7 +22,7 @@
 def kernel(
     emb, w, gain, sdown, sup, tasks, alloc, lens, cot,
     hidden, grads_in, gdown, gup,
-    wbuf, xbuf, obuf, hbuf, gbuf, gout, down, up, lowbuf, invbuf, mixb, mixrow, seq, got,
+    wbuf, xbuf, obuf, hbuf, gbuf, gout, down, up, lowbuf, invbuf, mixb, table, acc, seq, got,
     first_s, first_r, second_s, second_r, own_sem,
     x_s, x_r, g_s, g_r, load_sem, store_sem, seq_s, seq_r,
 ):
@@ -84,6 +84,8 @@
         c.start()
         own.append(c)
 
+    pltpu.make_async_copy(alloc, table, load_sem.at[2]).start()
+
     @pl.when(seg == 0)
     def _():
         pltpu.make_async_copy(emb, xbuf, load_sem.at[0]).start()
@@ -92,13 +94,14 @@
     def _():
         pltpu.make_async_copy(cot, gbuf, load_sem.at[1]).start()
 
-    table = alloc[...].astype(F32).astype(BF16)
-    total = alloc.shape[0]
-    picked = (tasks[...] == lax.broadcasted_iota(jnp.int32, (tasks.shape[0], total), 1)).astype(F32).astype(BF16)
-    uses = dot(picked, table)
-    mix = uses / jnp.maximum(jnp.sum(uses, axis=1, keepdims=True), 1.0)
-    for s in range(skills):
-        mixb[s] = jnp.broadcast_to(mix[:, s : s + 1], mixb.shape[1:])
+    pltpu.make_async_copy(alloc, table, load_sem.at[2]).wait()
+    known = table[...].astype(F32).astype(BF16)
+    for m in range(micro):
+        picked = lax.broadcasted_iota(jnp.int32, (table.shape[0], members), 0) == tasks[m : m + 1, :]
+        uses = dot(picked.astype(F32).astype(BF16), known, ((0,), (0,)))
+        mix = uses / jnp.maximum(jnp.sum(uses, axis=1, keepdims=True), 1.0)
+        for s in range(skills):
+            mixb[s, m * members : (m + 1) * members] = jnp.broadcast_to(mix[:, s : s + 1], (members, mixb.shape[2]))
     step = mixb.shape[2]
 
     def adapters(i, c):
@@ -156,120 +159,23 @@
                 second[h][i][d].wait_send()
 
     wide = width // CHUNKS
-    tile = 512
+
+    def chunk(q):
+        return pl.ds(pl.multiple_of(q * wide, wide), wide)
+
+    def by_columns(q):
+        return wbuf[q // (CHUNKS // 2), :, chunk(lax.rem(q, CHUNKS // 2))]
 
     def hop(buf, target, m, q, s, r, to):
-        cols = pl.ds(q * wide, wide)
         return pltpu.make_async_remote_copy(
-            src_ref=buf.at[m, :, cols], dst_ref=target.at[m, :, cols], send_sem=s.at[m, q], recv_sem=r.at[m, q],
+            src_ref=buf.at[m, :, chunk(q)], dst_ref=target.at[m, :, chunk(q)], send_sem=s.at[m, q], recv_sem=r.at[m, q],
             device_id=(to, me), device_id_type=MESH,
         )
 
     onward = functools.partial(hop, obuf, xbuf, s=x_s, r=x_r, to=lax.rem(seg + 1, segments))
     back = functools.partial(hop, gout, gbuf, s=g_s, r=g_r, to=lax.rem(seg + last, segments))
-
-    @pl.when(seg == 0)
-    def _():
-        pltpu.make_async_copy(emb, xbuf, load_sem.at[0]).wait()
-
-    for m in range(micro):
-
-        @pl.when(seg > 0)
-        def _():
-            for q in range(CHUNKS):
-                onward(m, q).wait_recv()
-
-        def squares(i, acc):
-            v = xbuf[m, :, pl.ds(pl.multiple_of(i * tile, tile), tile)].astype(F32)
-            return acc + jnp.sum(v * v, axis=1, keepdims=True)
-
-        ss = lax.fori_loop(0, width // tile, squares, jnp.zeros((rows, 1), F32))
-        inv = lax.rsqrt(ss / width + EPS)
-        invbuf[m] = inv
-
-        def normed(i, c):
-            cols = pl.ds(pl.multiple_of(i * tile, tile), tile)
-            hbuf[m, :, cols] = (xbuf[m, :, cols].astype(F32) * inv * gain[:, cols]).astype(BF16)
-            return c
-
-        lax.fori_loop(0, width // tile, normed, 0)
-        low = dot(hbuf[m], down[m], ((1,), (1,))).astype(BF16)
-        lowbuf[m] = low
-        for q in range(CHUNKS):
-
-            def forward(i, c):
-                at_col = q * wide + i * tile
-                cols = pl.ds(pl.multiple_of(at_col, tile), tile)
-                inner = pl.ds(pl.multiple_of(at_col - (q * wide // half) * half, tile), tile)
-                acc = dot(hbuf[m], wbuf[q * wide // half, :, inner])
-                acc = acc + dot(low, up[m, :, cols])
-                obuf[m, :, cols] = (xbuf[m, :, cols].astype(F32) + acc).astype(BF16)
-                return c
-
-            lax.fori_loop(0, wide // tile, forward, 0)
-
-            @pl.when(seg < last)
-            def _():
-                onward(m, q).start()
-
-        pltpu.make_async_copy(obuf.at[m], hidden.at[m], store_sem.at[m]).start()
-
-    @pl.when(seg == last)
-    def _():
-        pltpu.make_async_copy(cot, gbuf, load_sem.at[1]).wait()
-        for m in range(micro):
-            keep = lax.broadcasted_iota(jnp.int32, (rows, tile), 0) < lens[m, me]
-
-            def masked(i, c):
-                cols = pl.ds(pl.multiple_of(i * tile, tile), tile)
-                gbuf[m, :, cols] = jnp.where(keep, gbuf[m, :, cols].astype(F32), 0.0).astype(BF16)
-                return c
-
-            lax.fori_loop(0, width // tile, masked, 0)
-
-    btile = 256
-    for m in range(micro):
-
-        @pl.when(seg < last)
-        def _():
-            for q in range(CHUNKS):
-                back(m, q).wait_recv()
-
-        glow = dot(gbuf[m], up[m], ((1,), (1,))).astype(BF16)
-        inv = invbuf[m]
-
-        def along(i, acc):
-            cols = pl.ds(pl.multiple_of(i * tile, tile), tile)
-            step_out = obuf[m, :, cols].astype(F32) - xbuf[m, :, cols].astype(F32)
-            return acc + jnp.sum(gbuf[m, :, cols].astype(F32) * step_out, axis=1, keepdims=True)
-
-        coef = lax.fori_loop(0, width // tile, along, jnp.zeros((rows, 1), F32)) / width * inv * inv
-        for q in range(CHUNKS):
-
-            def backward(i, c):
-                cols = pl.ds(pl.multiple_of(q * wide + i * btile, btile), btile)
-                dh = dot(gbuf[m, :, :half], wbuf[0, cols, :], ((1,), (1,)))
-                dh = dh + dot(gbuf[m, :, half:], wbuf[1, cols, :], ((1,), (1,)))
-                dh = dh + dot(glow, down[m, :, cols])
-                out = gbuf[m, :, cols].astype(F32) + inv * (gain[:, cols] * dh) - xbuf[m, :, cols].astype(F32) * coef
-                gout[m, :, cols] = out.astype(BF16)
-                return c
-
-            lax.fori_loop(0, wide // btile, backward, 0)
-
-            @pl.when(seg > 0)
-            def _():
-                back(m, q).start()
-
-        pltpu.make_async_copy(gout.at[m], grads_in.at[m], store_sem.at[micro + m]).start()
-
-        def adapter_grads(i, c):
-            cols = pl.ds(pl.multiple_of(i * tile, tile), tile)
-            seq[m, :, cols] = dot(glow, hbuf[m, :, cols], ((0,), (0,)))
-            seq[micro + m, :, cols] = dot(lowbuf[m], gbuf[m, :, cols], ((0,), (0,)))
-            return c
-
-        lax.fori_loop(0, width // tile, adapter_grads, 0)
+    column = jnp.zeros((rows, 1), F32)
+    narrow = jnp.zeros((rows, rank), F32)
 
     def share(d):
         to = lax.rem(me + d, members)
@@ -282,6 +188,193 @@
         share(d).start()
         return c
 
+    def over_chunks(body, init=0):
+        return lax.fori_loop(0, CHUNKS, body, init)
+
+    def forward(m, as_it_comes):
+        if as_it_comes:
+            acc[...] = jnp.zeros_like(acc)
+
+        def take_in(q, c):
+            ss, lw = c
+
+            @pl.when(seg > 0)
+            def _():
+                onward(m, q).wait_recv()
+
+            v = xbuf[m, :, chunk(q)].astype(F32)
+            h = (v * gain[:, chunk(q)]).astype(BF16)
+            if as_it_comes:
+                for i in range(2):
+                    acc[:, i * half : (i + 1) * half] += dot(h, wbuf[i, chunk(q), :])
+            else:
+                hbuf[m, :, chunk(q)] = h
+            return ss + jnp.sum(v * v, axis=1, keepdims=True), lw + dot(h, down[m, :, chunk(q)], ((1,), (1,)))
+
+        ss, lw = over_chunks(take_in, (column, narrow))
+        inv = lax.rsqrt(ss / width + EPS)
+        low = (lw * inv).astype(BF16)
+        invbuf[m] = inv
+        lowbuf[m] = low
+
+        def give_out(q, c):
+            total = acc[:, chunk(q)] if as_it_comes else dot(hbuf[m], by_columns(q))
+            total = xbuf[m, :, chunk(q)].astype(F32) + inv * total + dot(low, up[m, :, chunk(q)])
+            obuf[m, :, chunk(q)] = total.astype(BF16)
+
+            @pl.when(seg < last)
+            def _():
+                onward(m, q).start()
+
+            return c
+
+        over_chunks(give_out)
+        pltpu.make_async_copy(obuf.at[m], hidden.at[m], store_sem.at[m]).start()
+
+    def normed(m):
+        def body(q, c):
+            h = xbuf[m, :, chunk(q)].astype(F32) * invbuf[m] * gain[:, chunk(q)]
+            hbuf[m, :, chunk(q)] = h.astype(BF16)
+            return c
+
+        over_chunks(body)
+
+    def backward(m, kind):
+        if kind == "comes":
+            acc[...] = jnp.zeros_like(acc)
+
+        def take_in(q, c):
+            along, gl = c
+
+            @pl.when(seg < last)
+            def _():
+                back(m, q).wait_recv()
+
+            g = gbuf[m, :, chunk(q)]
+            if kind == "comes":
+                for i in range(2):
+                    acc[:, i * half : (i + 1) * half] += dot(g, wbuf[i, chunk(q), :])
+            change = obuf[m, :, chunk(q)].astype(F32) - xbuf[m, :, chunk(q)].astype(F32)
+            along = along + jnp.sum(g.astype(F32) * change, axis=1, keepdims=True)
+            return along, gl + dot(g, up[m, :, chunk(q)], ((1,), (1,)))
+
+        along, gl = over_chunks(take_in, (column, narrow))
+        glow = gl.astype(BF16)
+        inv = invbuf[m]
+        coef = along / width * inv * inv
+
+        def adapter_grads():
+            def body(q, c):
+                seq[m, :, chunk(q)] = dot(glow, hbuf[m, :, chunk(q)], ((0,), (0,)))
+                seq[micro + m, :, chunk(q)] = dot(lowbuf[m], gbuf[m, :, chunk(q)], ((0,), (0,)))
+                return c
+
+            over_chunks(body)
+
+            @pl.when(m == micro - 1)
+            def _():
+                lax.fori_loop(1, members, share_start, 0)
+
+        @pl.when(seg == 0)
+        def _():
+            adapter_grads()
+
+        def give_out(q, c):
+            if kind == "comes":
+                dh = acc[:, chunk(q)]
+            elif kind == "columns":
+                dh = dot(gbuf[m], by_columns(q))
+            else:
+                dh = dot(gbuf[m, :, :half], wbuf[0, chunk(q), :], ((1,), (1,)))
+                dh = dh + dot(gbuf[m, :, half:], wbuf[1, chunk(q), :], ((1,), (1,)))
+            dh = dh + dot(glow, down[m, :, chunk(q)])
+            out = gbuf[m, :, chunk(q)].astype(F32) + inv * (gain[:, chunk(q)] * dh)
+            gout[m, :, chunk(q)] = (out - xbuf[m, :, chunk(q)].astype(F32) * coef).astype(BF16)
+
+            @pl.when(seg > 0)
+            def _():
+                back(m, q).start()
+
+            return c
+
+        over_chunks(give_out)
+        pltpu.make_async_copy(gout.at[m], grads_in.at[m], store_sem.at[micro + m]).start()
+
+        @pl.when(seg > 0)
+        def _():
+            adapter_grads()
+
+    def each_micro(body):
+        def step(m, c):
+            body(m)
+            return c
+
+        lax.fori_loop(0, micro, step, 0)
+
+    even = lax.rem(seg, 2) == 0
+
+    @pl.when(seg == 0)
+    def _():
+        pltpu.make_async_copy(emb, xbuf, load_sem.at[0]).wait()
+
+    @pl.when(even)
+    def _():
+        each_micro(lambda m: forward(m, True))
+
+    @pl.when(jnp.logical_not(even) & (seg < last))
+    def _():
+        each_micro(lambda m: forward(m, False))
+
+    @pl.when(seg < last)
+    def _():
+        each_micro(normed)
+
+        size = 512
+        count = width // size
+
+        def place(i, j):
+            inner = lax.rem(j, count // 2)
+            return wbuf.at[
+                j // (count // 2), pl.ds(pl.multiple_of(i * size, size), size), pl.ds(pl.multiple_of(inner * size, size), size)
+            ]
+
+        def turn(i, c):
+            def inner(j, c):
+                a, b = place(i, j)[...].T, place(j, i)[...].T
+                place(j, i)[...] = a
+                place(i, j)[...] = b
+                return c
+
+            return lax.fori_loop(i, count, inner, c)
+
+        lax.fori_loop(0, count, turn, 0)
+
+    @pl.when(even)
+    def _():
+        each_micro(lambda m: backward(m, "columns"))
+
+    @pl.when(jnp.logical_not(even) & (seg < last))
+    def _():
+        each_micro(lambda m: backward(m, "comes"))
+
+    @pl.when(seg == last)
+    def _():
+        pltpu.make_async_copy(cot, gbuf, load_sem.at[1]).wait()
+
+        def both(m):
+            keep = lax.broadcasted_iota(jnp.int32, (rows, wide), 0) < lens[m, me]
+
+            def masked(q, c):
+                gbuf[m, :, chunk(q)] = jnp.where(keep, gbuf[m, :, chunk(q)].astype(F32), 0.0).astype(BF16)
+                return c
+
+            over_chunks(masked)
+            forward(m, False)
+            normed(m)
+            backward(m, "rows")
+
+        each_micro(both)
+
     def add(mine, source, fresh):
         for t, target in enumerate((gdown, gup)):
             for s in range(skills):
@@ -289,7 +382,6 @@
                 p = p.astype(BF16).astype(F32)
                 target[s] = p if fresh else target[s] + p
 
-    lax.fori_loop(1, members, share_start, 0)
     own_cols = pl.ds(pl.multiple_of(me * block, block), block)
     add([seq[i, :, own_cols] for i in range(2 * micro)], me, True)
 
@@ -337,7 +429,7 @@
     hidden, grads_in, gdown, gup = pl.pallas_call(
         kernel,
         out_shape=(stream, stream, grad, grad),
-        in_specs=[anywhere, anywhere, vmem, vmem, vmem, vmem, vmem, smem, anywhere],
+        in_specs=[anywhere, anywhere, vmem, vmem, vmem, vmem, anywhere, smem, anywhere],
         out_specs=(anywhere, anywhere, vmem, vmem),
         scratch_shapes=[
             pltpu.VMEM((2, width, width // 2), BF16),
@@ -347,19 +439,20 @@
             pltpu.VMEM((micro, rows, rank), BF16),
             pltpu.VMEM((micro, rows, 1), F32),
             pltpu.VMEM((skills, micro * members, block), F32),
-            pltpu.VMEM((8, 128), F32),
+            pltpu.VMEM(allocation.shape, jnp.int32),
+            pltpu.VMEM((rows, width), F32),
             pltpu.VMEM((2 * micro, rank, width), F32),
             pltpu.VMEM((members, 2 * micro, rank, block), F32),
             dma((2, 4)), dma((2, 4)), dma((2, 4, 4)), dma((2, 4, 4)), dma((2,)),
             dma((micro, CHUNKS)), dma((micro, CHUNKS)), dma((micro, CHUNKS)), dma((micro, CHUNKS)),
-            dma((2,)), dma((2 * micro,)), dma((members,)), dma((members,)),
+            dma((3,)), dma((2 * micro,)), dma((members,)), dma((members,)),
         ],
         compiler_params=pltpu.CompilerParams(
             collective_id=0, has_side_effects=True, vmem_limit_bytes=60 * 1024 * 1024
         ),
     )(
         embeds[:, 0], base_weight[0], norm_gain, skill_down[0], skill_up[0],
-        task_ids.reshape(-1, 1), allocation, target_lengths, cotangent[:, 0],
+        task_ids, allocation, target_lengths, cotangent[:, 0],
     )
     return (hidden[None, :, None], grads_in[None, :, None], gdown[None], gup[None])
 

time: 462 us -> 362 us (0.78)
  Pallas kernels: 452 us -> 353 us
    pallas_call x1, Pallas kernels: 452 us -> 353 us  [shards(): pl.pallas_call(kernel, out_shape=(stream, stream, grad, grad), in_specs=[...]
where the time goes in v2:
time: 362 us; the launch traced here: 361 us
  Pallas kernels  353 us (98%)
  local copies, waits for them, and re-layouts  8.07 us (2%)
    pallas_call x1, Pallas kernels, shards(): pl.pallas_call(kernel, out_shape=(stream, stream, grad, grad), in_specs=[...  353 us
    unnamed x11, local copies, waits for them, and re-layouts  8.07 us

profile of v2, /device:TPU:0, one launch (start us, length us, event | category | flops | bytes accessed | tf_op | source)
XLA Modules:
  0.0 361.4 jit_solution(81507321011599641)
XLA Ops:
  0.6 2.2 copy.13.alloc
  2.8 352.7 %shard_map.120 = (bf16[2,128,4096]{2,1,0:T(8,128)(2,1)}, bf16[2,128,4096]{2,1,0:T(8,128)(2,1)}, f32[16,8,256]{2,1,0:T(8,128)}, f32[16,8,256]{2,1,0:T(8,128)}) custom-call(bf16[2,128,4096]{2,1,0:T(8,128)(2,1)} %bitcast.15, bf16[256,4096]{1,0:T(8,128)(2,1)} %bitcast.16, f32[1,4096]{1,0:T(1,128)} %gain.1, bf16[16,8,4096]{2,1,0:T(8,128)(2,1)} %bitcast.18, ...), custom_call_target="tpu_custom_call" | custom-call | tf_op jit(solution)/shard_map/pallas_call | solution.py:429
  355.5 0.0 copy-start
  355.5 3.3 copy.20
  358.8 0.0 copy-done
  358.8 0.0 copy-start.2
  358.8 0.0 copy-start.1
  358.8 1.3 copy.21
  360.1 0.0 copy-done.2
  360.1 0.7 copy.22
  360.7 0.0 copy-done.1
  360.7 0.7 copy.23
Async XLA Ops:
  355.5 3.3 copy-start
  358.8 1.3 copy-start.2
  358.8 2.0 copy-start.1

commit v3 on v2

v3 whole, which is shorter than its diff:
```python
import functools

import jax
import jax.numpy as jnp
from jax import lax
from jax.experimental import pallas as pl
from jax.experimental.pallas import tpu as pltpu
from jax.sharding import PartitionSpec as P

EPS = 1e-06
MESH = pl.DeviceIdType.MESH
SIDE = 4
CHUNKS = 8
F32 = jnp.float32
BF16 = jnp.bfloat16


def dot(a, b, dims=((1,), (0,))):
    return lax.dot_general(a, b, (dims, ((), ())), preferred_element_type=F32)


def kernel(
    emb, w, gain, sdown, sup, tasks, alloc, lens, cot,
    hidden, grads_in, gdown, gup,
    wbuf, vis, xbuf, obuf, hbuf, gbuf, gout, down, up, lowbuf, glowbuf, invbuf, mixb, table, acc, seq, got,
    *sems,
):
    main_sems, rest_sems, visit_sems = sems[:4], sems[4:8], sems[8:12]
    over_s, over_r, back_s, back_r, own_sem = sems[12:17]
    x_s, x_r, g_s, g_r, load_sem, store_sem, seq_s, seq_r = sems[17:]
    segments = lax.axis_size("segment")
    members = lax.axis_size("dp")
    seg = lax.axis_index("segment")
    me = lax.axis_index("dp")
    micro, rows, width = emb.shape
    block = w.shape[0]
    half = width // 2
    part = block // 2
    skills, rank = sdown.shape[0], sdown.shape[1]
    z, y = me // SIDE, lax.rem(me, SIDE)
    last = segments - 1

    barrier = pltpu.get_barrier_semaphore()

    def greet(d, c):
        pl.semaphore_signal(barrier, inc=1, device_id=(seg, lax.rem(me + d, members)), device_id_type=MESH)
        return c

    lax.fori_loop(1, members, greet, 0)
    for d in (1, 2, segments - 2, segments - 1):
        pl.semaphore_signal(barrier, inc=1, device_id=(lax.rem(seg + d, segments), me), device_id_type=MESH)
    pl.semaphore_wait(barrier, members + 3)

    wide = width // CHUNKS

    def chunk(q):
        return pl.ds(pl.multiple_of(q * wide, wide), wide)

    def by_columns(q):
        return wbuf[q // (CHUNKS // 2), :, chunk(lax.rem(q, CHUNKS // 2))]

    def hop(buf, target, m, q, s, r, to):
        return pltpu.make_async_remote_copy(
            src_ref=buf.at[m, :, chunk(q)], dst_ref=target.at[m, :, chunk(q)], send_sem=s.at[m, q], recv_sem=r.at[m, q],
            device_id=(to, me), device_id_type=MESH,
        )

    onward = functools.partial(hop, obuf, xbuf, s=x_s, r=x_r, to=lax.rem(seg + 1, segments))
    back = functools.partial(hop, gout, gbuf, s=g_s, r=g_r, to=lax.rem(seg + last, segments))
    column = jnp.zeros((rows, 1), F32)
    narrow = jnp.zeros((rows, rank), F32)

    def share(d):
        to = lax.rem(me + d, members)
        return pltpu.make_async_remote_copy(
            src_ref=seq.at[:, :, pl.ds(pl.multiple_of(to * block, block), block)], dst_ref=got.at[d],
            send_sem=seq_s.at[d], recv_sem=seq_r.at[d], device_id=(seg, to), device_id_type=MESH,
        )

    def share_start(d, c):
        share(d).start()
        return c

    def over_chunks(body, init=0):
        return lax.fori_loop(0, CHUNKS, body, init)

    def each_micro(body):
        def step(m, c):
            body(m)
            return c

        lax.fori_loop(0, micro, step, 0)

    def begin(m, kind):
        if kind == "comes":
            acc[m] = jnp.zeros((rows, width), F32)

        def take_in(q, c):
            ss, lw = c
            if kind != "early":

                @pl.when(seg > 0)
                def _():
                    onward(m, q).wait_recv()

            v = xbuf[m, :, chunk(q)].astype(F32)
            h = (v * gain[:, chunk(q)]).astype(BF16)
            if kind == "comes":
                for i in range(2):
                    acc[m, :, i * half : (i + 1) * half] += dot(h, wbuf[i, chunk(q), :])
            else:
                hbuf[m, :, chunk(q)] = h
            return ss + jnp.sum(v * v, axis=1, keepdims=True), lw + dot(h, down[m, :, chunk(q)], ((1,), (1,)))

        ss, lw = over_chunks(take_in, (column, narrow))
        inv = lax.rsqrt(ss / width + EPS)
        invbuf[m] = inv
        lowbuf[m] = (lw * inv).astype(BF16)

    def finish(m, kind):
        inv = invbuf[m]
        low = lowbuf[m]

        def give_out(q, c):
            total = dot(hbuf[m], by_columns(q)) if kind == "columns" else acc[m, :, chunk(q)]
            total = xbuf[m, :, chunk(q)].astype(F32) + inv * total + dot(low, up[m, :, chunk(q)])
            obuf[m, :, chunk(q)] = total.astype(BF16)

            @pl.when(seg < last)
            def _():
                onward(m, q).start()

            return c

        over_chunks(give_out)
        pltpu.make_async_copy(obuf.at[m], hidden.at[m], store_sem.at[m]).start()

    def forward(m, kind):
        begin(m, kind)
        finish(m, kind)

    extra = vis.shape[2]
    most = half - extra
    order = (0, -1, 1, 2)
    ways = (1, -1)
    opening = seg < 2
    closing = seg >= segments - 2

    def at(h, df, ds):
        dy, dz = (df, ds) if h == 0 else (ds, df)
        return lax.rem(z + dz + SIDE, SIDE) * SIDE + lax.rem(y + dy + SIDE, SIDE)

    def block_of(buf, cols, h, df, ds, sub=None):
        start = at(h, df, ds) * block
        if sub is None:
            return buf.at[h, pl.ds(pl.multiple_of(start, block), block), cols]
        return buf.at[h, pl.ds(pl.multiple_of(start + sub * part, part), part), cols]

    def remote(src, dst, s, r, to, to_seg=seg):
        return pltpu.make_async_remote_copy(
            src_ref=src, dst_ref=dst, send_sem=s, recv_sem=r, device_id=(to_seg, to), device_id_type=MESH
        )

    class Stream:
        def __init__(self, buf, cols, mine, f_s, f_r, s_s, s_r):
            self.ref = functools.partial(block_of, buf, cols)
            self.mine, self.sems = mine, (f_s, f_r, s_s, s_r)

        def first(self, h, d):
            way = ways[d % 2]
            dst = self.ref(h, 0, 0) if d < 2 else self.ref(h, -way, 0, d - 2)
            src = self.mine(h) if d < 2 else dst
            return remote(src, dst, self.sems[0].at[h, d], self.sems[1].at[h, d], at(h, way, 0))

        def second(self, h, i, d):
            way = ways[d % 2]
            dst = self.ref(h, order[i], 0) if d < 2 else self.ref(h, order[i], -way, d - 2)
            src = self.mine(h) if d < 2 and i == 0 else dst
            return remote(src, dst, self.sems[2].at[h, i, d], self.sems[3].at[h, i, d], at(h, 0, way))

        def open(self):
            for h in range(2):
                for d in range(2):
                    self.first(h, d).start()
            for h in range(2):
                self.spread(h, 0)

        def arrived_first(self, h):
            for d in range(2):
                self.first(h, d).wait_recv()
                self.first(h, 2 + d).start()

        def spread(self, h, i):
            for d in range(2):
                self.second(h, i, d).start()

        def pass_on(self, h, i):
            for d in range(2):
                self.second(h, i, d).wait_recv()
                self.second(h, i, 2 + d).start()

        def first_done(self, h):
            for d in range(2):
                self.first(h, 2 + d).wait_recv()

        def second_done(self, h, i):
            for d in range(2):
                self.second(h, i, 2 + d).wait_recv()

        def sent(self):
            for h in range(2):
                for d in range(4):
                    self.first(h, d).wait_send()
                    for i in range(4):
                        self.second(h, i, d).wait_send()

    side = pl.ds(most, extra)
    main = Stream(wbuf, pl.ds(0, most), lambda h: w.at[:, pl.ds(h * half, most)], *main_sems)
    rest = Stream(wbuf, side, lambda h: w.at[:, pl.ds(h * half + most, extra)], *rest_sems)
    visit = Stream(vis, pl.ds(0, extra), lambda h: block_of(vis, pl.ds(0, extra), h, 0, 0), *visit_sems)

    def go_over(h):
        return remote(
            w.at[:, pl.ds(h * half + most, extra)], block_of(vis, pl.ds(0, extra), h, 0, 0),
            over_s.at[h], over_r.at[h], me, lax.rem(seg + segments - 2, segments),
        )

    def come_back(h, i, j):
        return remote(
            block_of(vis, pl.ds(0, extra), h, order[i], order[j]), block_of(wbuf, side, h, order[i], order[j]),
            back_s.at[h, i * 4 + j], back_r.at[h, i * 4 + j], me, lax.rem(seg + 2, segments),
        )

    def on_all_but_opening(body):
        pl.when(jnp.logical_not(opening))(body)

    def start_own():
        main.open()
        on_all_but_opening(rest.open)

    @pl.when(opening)
    def _():
        for h in range(2):
            go_over(h).start()

    @pl.when(jnp.logical_not(closing))
    def _():
        start_own()

    own = []
    for h in range(2):
        c = pltpu.make_async_copy(
            w.at[:, h * half : (h + 1) * half], block_of(wbuf, pl.ds(0, half), h, 0, 0), own_sem.at[h]
        )
        c.start()
        own.append(c)
    pltpu.make_async_copy(alloc, table, load_sem.at[2]).start()

    @pl.when(seg == 0)
    def _():
        pltpu.make_async_copy(emb, xbuf, load_sem.at[0]).start()

    @pl.when(seg == last)
    def _():
        pltpu.make_async_copy(cot, gbuf, load_sem.at[1]).start()


    @pl.when(closing)
    def _():
        for h in range(2):
            go_over(h).wait_recv()
        visit.open()
        for h in range(2):
            visit.arrived_first(h)
        for h in range(2):
            visit.spread(h, 1)
            visit.spread(h, 2)
        for h in range(2):
            come_back(h, 1, 0).start()
            come_back(h, 2, 0).start()
            visit.pass_on(h, 0)
        for h in range(2):
            visit.first_done(h)
            visit.spread(h, 3)
        start_own()
        for i in range(4):
            for h in range(2):
                if i > 0:
                    visit.pass_on(h, i)
                come_back(h, i, 1).start()
                come_back(h, i, 2).start()
        for h in range(2):
            come_back(h, 3, 0).start()
        for i in range(4):
            for h in range(2):
                visit.second_done(h, i)
                come_back(h, i, 3).start()

    pltpu.make_async_copy(alloc, table, load_sem.at[2]).wait()
    known = table[...].astype(F32).astype(BF16)
    for m in range(micro):
        picked = lax.broadcasted_iota(jnp.int32, (table.shape[1], members), 0) == tasks[m : m + 1, :]
        uses = dot(picked.astype(F32).astype(BF16), known, ((0,), (1,)))
        mix = uses / jnp.maximum(jnp.sum(uses, axis=1, keepdims=True), 1.0)
        for s in range(skills):
            mixb[s, m * members : (m + 1) * members] = jnp.broadcast_to(mix[:, s : s + 1], (members, mixb.shape[2]))
    step = mixb.shape[2]

    def adapters(i, c):
        cols = pl.ds(pl.multiple_of(i * step, step), step)
        for m in range(micro):
            for source, target in ((sdown, down), (sup, up)):
                acc = jnp.zeros((rank, step), F32)
                for s in range(skills):
                    acc = acc + mixb[s, pl.ds(m * members + me, 1), :] * source[s, :, cols].astype(F32)
                target[m, :, cols] = acc.astype(BF16)
        return c

    lax.fori_loop(0, width // step, adapters, 0)

    @pl.when(seg == 0)
    def _():
        pltpu.make_async_copy(emb, xbuf, load_sem.at[0]).wait()
        each_micro(lambda m: begin(m, "early"))
        acc[...] = jnp.zeros_like(acc)

    def used(df, ds, hs=(0, 1)):
        @pl.when(seg == 0)
        def _():
            for h in hs:
                start = pl.multiple_of(at(h, df, ds) * block, block)
                for m in range(micro):
                    acc[m, :, h * half : h * half + most] += dot(
                        hbuf[m, :, pl.ds(start, block)], wbuf[h, pl.ds(start, block), :most]
                    )

    def everywhere(step, *which):
        getattr(main, step)(*which)
        on_all_but_opening(lambda: getattr(rest, step)(*which))

    for h in range(2):
        everywhere("arrived_first", h)
    for h in range(2):
        everywhere("spread", h, 1)
        everywhere("spread", h, 2)
    for h in range(2):
        own[h].wait()
    used(0, 0)
    used(-1, 0)
    used(1, 0)
    for h in range(2):
        everywhere("pass_on", h, 0)
    for h in range(2):
        everywhere("first_done", h)
        everywhere("spread", h, 3)
    used(2, 0)
    for i in range(4):
        if i > 0:
            for h in range(2):
                everywhere("pass_on", h, i)
        used(order[i], -1)
        used(order[i], 1)

    @pl.when(opening)
    def _():
        for h in range(2):
            for i in range(4):
                for j in range(4):
                    if i + j > 0:
                        come_back(h, i, j).wait_recv()
            go_over(h).wait_send()

    @pl.when(seg == 0)
    def _():
        for h in range(2):
            for m in range(micro):
                acc[m, :, h * half + most : (h + 1) * half] = dot(hbuf[m], wbuf[h, :, most:])

    for i in range(4):
        for h in range(2):
            everywhere("second_done", h, i)
            used(order[i], 2, (h,))

    @pl.when(seg == 0)
    def _():
        each_micro(lambda m: finish(m, "early"))

    everywhere("sent")

    @pl.when(closing)
    def _():
        visit.sent()
        for h in range(2):
            for i in range(4):
                for j in range(4):
                    if i + j > 0:
                        come_back(h, i, j).wait_send()

    def normed(m):
        def body(q, c):
            h = xbuf[m, :, chunk(q)].astype(F32) * invbuf[m] * gain[:, chunk(q)]
            hbuf[m, :, chunk(q)] = h.astype(BF16)
            return c

        over_chunks(body)

    def adapter_grads(m):
        glow = glowbuf[m]

        def body(q, c):
            seq[m, :, chunk(q)] = dot(glow, hbuf[m, :, chunk(q)], ((0,), (0,)))
            seq[micro + m, :, chunk(q)] = dot(lowbuf[m], gbuf[m, :, chunk(q)], ((0,), (0,)))
            return c

        over_chunks(body)

    def share_all():
        lax.fori_loop(1, members, share_start, 0)

    def backward(m, kind, between=None):
        if kind == "comes":
            acc[m] = jnp.zeros((rows, width), F32)

        def take_in(q, c):
            along, gl = c
            if kind != "rows":
                back(m, q).wait_recv()
            g = gbuf[m, :, chunk(q)]
            if kind == "comes":
                for i in range(2):
                    acc[m, :, i * half : (i + 1) * half] += dot(g, wbuf[i, chunk(q), :])
            change = obuf[m, :, chunk(q)].astype(F32) - xbuf[m, :, chunk(q)].astype(F32)
            along = along + jnp.sum(g.astype(F32) * change, axis=1, keepdims=True)
            return along, gl + dot(g, up[m, :, chunk(q)], ((1,), (1,)))

        along, gl = over_chunks(take_in, (column, narrow))
        glow = gl.astype(BF16)
        glowbuf[m] = glow
        inv = invbuf[m]
        coef = along / width * inv * inv
        if between is not None:

            @pl.when(seg == 0)
            def _():
                between(m)

        at_once = 2 if kind == "rows" else 1

        def give_out(q, c):
            cols = pl.ds(pl.multiple_of(q * at_once * wide, at_once * wide), at_once * wide)
            if kind == "comes":
                dh = acc[m, :, cols]
            elif kind == "columns":
                dh = dot(gbuf[m], by_columns(q))
            else:
                turned = dot(wbuf[0, cols, :], gbuf[m, :, :half], ((1,), (1,)))
                turned = turned + dot(wbuf[1, cols, :], gbuf[m, :, half:], ((1,), (1,)))
                dh = turned.T
            dh = dh + dot(glow, down[m, :, cols])
            out = gbuf[m, :, cols].astype(F32) + inv * (gain[:, cols] * dh)
            gout[m, :, cols] = (out - xbuf[m, :, cols].astype(F32) * coef).astype(BF16)

            @pl.when(seg > 0)
            def _():
                for i in range(at_once):
                    back(m, q * at_once + i).start()

            return c

        lax.fori_loop(0, CHUNKS // at_once, give_out, 0)
        pltpu.make_async_copy(gout.at[m], grads_in.at[m], store_sem.at[micro + m]).start()

    even = lax.rem(seg, 2) == 0

    @pl.when(even & (seg > 0))
    def _():
        each_micro(lambda m: forward(m, "comes"))

    @pl.when(jnp.logical_not(even) & (seg < last))
    def _():
        each_micro(lambda m: forward(m, "columns"))

    @pl.when(seg < last)
    def _():
        each_micro(normed)

        size = 512
        count = width // size

        def place(i, j):
            inner = lax.rem(j, count // 2)
            return wbuf.at[
                j // (count // 2), pl.ds(pl.multiple_of(i * size, size), size), pl.ds(pl.multiple_of(inner * size, size), size)
            ]

        def turn(i, c):
            def inner(j, c):
                a, b = place(i, j)[...].T, place(j, i)[...].T
                place(j, i)[...] = a
                place(i, j)[...] = b
                return c

            return lax.fori_loop(i, count, inner, c)

        lax.fori_loop(0, count, turn, 0)

    def before_the_last(m):
        adapter_grads(m)

        @pl.when(m == micro - 1)
        def _():
            share_all()

    @pl.when(even)
    def _():
        each_micro(lambda m: backward(m, "columns", before_the_last))

    @pl.when(jnp.logical_not(even) & (seg < last))
    def _():
        each_micro(lambda m: backward(m, "comes"))

    @pl.when(seg == last)
    def _():
        pltpu.make_async_copy(cot, gbuf, load_sem.at[1]).wait()

        def both(m):
            keep = lax.broadcasted_iota(jnp.int32, (rows, wide), 0) < lens[m, me]

            def masked(q, c):
                gbuf[m, :, chunk(q)] = jnp.where(keep, gbuf[m, :, chunk(q)].astype(F32), 0.0).astype(BF16)
                return c

            over_chunks(masked)
            forward(m, "columns")
            backward(m, "rows")

        each_micro(both)
        each_micro(normed)

    @pl.when(seg > 0)
    def _():
        each_micro(adapter_grads)
        share_all()

    def add(mine, source, fresh):
        for t, target in enumerate((gdown, gup)):
            for s in range(skills):
                p = sum(mixb[s, pl.ds(m * members + source, 1), :] * mine[t * micro + m] for m in range(micro))
                p = p.astype(BF16).astype(F32)
                target[s] = p if fresh else target[s] + p

    own_cols = pl.ds(pl.multiple_of(me * block, block), block)
    add([seq[i, :, own_cols] for i in range(2 * micro)], me, True)

    def take(d, c):
        share(d).wait_recv()
        add([got[d, i] for i in range(2 * micro)], lax.rem(me - d + members, members), False)
        return c

    lax.fori_loop(1, members, take, 0)

    def drain(d, c):
        share(d).wait_send()
        return c

    lax.fori_loop(1, members, drain, 0)
    for m in range(micro):
        pltpu.make_async_copy(obuf.at[m], hidden.at[m], store_sem.at[m]).wait()
        pltpu.make_async_copy(gout.at[m], grads_in.at[m], store_sem.at[micro + m]).wait()

    @pl.when(seg < last)
    def _():
        for m in range(micro):
            for q in range(CHUNKS):
                onward(m, q).wait_send()

    @pl.when(seg > 0)
    def _():
        for m in range(micro):
            for q in range(CHUNKS):
                back(m, q).wait_send()


def shards(embeds, base_weight, norm_gain, skill_down, skill_up, task_ids, allocation, target_lengths, cotangent):
    micro, _, rows, width = embeds.shape
    block = base_weight.shape[1]
    _, skills, rank, _ = skill_down.shape
    members = lax.axis_size("dp")
    anywhere = pl.BlockSpec(memory_space=pl.ANY)
    vmem = pl.BlockSpec(memory_space=pltpu.VMEM)
    smem = pl.BlockSpec(memory_space=pltpu.SMEM)
    stream = jax.ShapeDtypeStruct((micro, rows, width), BF16)
    grad = jax.ShapeDtypeStruct((skills, rank, block), F32)
    dma = pltpu.SemaphoreType.DMA
    held = pltpu.VMEM((micro, rows, width), BF16)
    hidden, grads_in, gdown, gup = pl.pallas_call(
        kernel,
        out_shape=(stream, stream, grad, grad),
        in_specs=[anywhere, anywhere, vmem, vmem, vmem, vmem, anywhere, smem, anywhere],
        out_specs=(anywhere, anywhere, vmem, vmem),
        scratch_shapes=[
            pltpu.VMEM((2, width, width // 2), BF16),
            pltpu.VMEM((2, width, width // 16), BF16),
            held, held, held, held, held,
            pltpu.VMEM((micro, rank, width), BF16),
            pltpu.VMEM((micro, rank, width), BF16),
            pltpu.VMEM((micro, rows, rank), BF16),
            pltpu.VMEM((micro, rows, rank), BF16),
            pltpu.VMEM((micro, rows, 1), F32),
            pltpu.VMEM((skills, micro * members, block), F32),
            pltpu.VMEM(allocation.shape[::-1], jnp.int32),
            pltpu.VMEM((micro, rows, width), F32),
            pltpu.VMEM((2 * micro, rank, width), F32),
            pltpu.VMEM((members, 2 * micro, rank, block), F32),
            *((dma((2, 4)), dma((2, 4)), dma((2, 4, 4)), dma((2, 4, 4))) * 3),
            dma((2,)), dma((2,)), dma((2, 16)), dma((2, 16)), dma((2,)),
            dma((micro, CHUNKS)), dma((micro, CHUNKS)), dma((micro, CHUNKS)), dma((micro, CHUNKS)),
            dma((3,)), dma((2 * micro,)), dma((members,)), dma((members,)),
        ],
        compiler_params=pltpu.CompilerParams(
            collective_id=0, has_side_effects=True, vmem_limit_bytes=60 * 1024 * 1024
        ),
    )(
        embeds[:, 0], base_weight[0], norm_gain, skill_down[0], skill_up[0],
        task_ids, allocation.T, target_lengths, cotangent[:, 0],
    )
    return (hidden[None, :, None], grads_in[None, :, None], gdown[None], gup[None])


def solution(mesh):
    in_specs = (
        P(None, "dp", None, None),
        P("segment", "dp", None),
        P("segment", None),
        P("segment", None, None, None),
        P("segment", None, None, None),
        P(),
        P(),
        P(),
        P(None, "dp", None, None),
    )
    out_specs = (
        P("segment", None, "dp", None, None),
        P("segment", None, "dp", None, None),
        P("segment", None, None, "dp"),
        P("segment", None, None, "dp"),
    )
    return jax.shard_map(shards, mesh=mesh, in_specs=in_specs, out_specs=out_specs, check_vma=False)
```

time: 362 us -> 339 us (0.936)
  Pallas kernels: 353 us -> 332 us
    pallas_call x1, Pallas kernels: 353 us -> 332 us  [shards(): pl.pallas_call(kernel, out_shape=(stream, stream, grad, grad), in_specs=[...]
    unnamed x11 -> x10, local copies, waits for them, and re-layouts: 8.07 us -> 5.92 us
where the time goes in v3:
time: 339 us
  Pallas kernels  332 us (98%)
  local copies, waits for them, and re-layouts  5.92 us (2%)
    pallas_call x1, Pallas kernels, shards(): pl.pallas_call(kernel, out_shape=(stream, stream, grad, grad), in_specs=[...  332 us

profile of v3, /device:TPU:0, one launch (start us, length us, event | category | flops | bytes accessed | tf_op | source)
XLA Modules:
  0.0 338.5 jit_solution(15007230884539244798)
XLA Ops:
  0.6 332.0 %shard_map.120 = (bf16[2,128,4096]{2,1,0:T(8,128)(2,1)}, bf16[2,128,4096]{2,1,0:T(8,128)(2,1)}, f32[16,8,256]{2,1,0:T(8,128)}, f32[16,8,256]{2,1,0:T(8,128)}) custom-call(bf16[2,128,4096]{2,1,0:T(8,128)(2,1)} %bitcast.16, bf16[256,4096]{1,0:T(8,128)(2,1)} %bitcast.17, f32[1,4096]{1,0:T(1,128)} %gain.1, bf16[16,8,4096]{2,1,0:T(8,128)(2,1)} %bitcast.19, ...), custom_call_target="tpu_custom_call" | custom-call | tf_op jit(solution)/shard_map/pallas_call | solution.py:596
  332.6 0.0 copy-start
  332.6 3.3 copy.19
  335.9 0.0 copy-done
  335.9 0.0 copy-start.2
  335.9 0.0 copy-start.1
  335.9 1.3 copy.20
  337.2 0.0 copy-done.2
  337.2 0.7 copy.21
  337.9 0.0 copy-done.1
  337.9 0.7 copy.22
Async XLA Ops:
  332.6 3.3 copy-start
  335.9 1.3 copy-start.2
  335.9 2.0 copy-start.1

commit v4 on v3

--- a/solution.py
+++ b/solution.py
@@ -27,7 +27,7 @@
 ):
     main_sems, rest_sems, visit_sems = sems[:4], sems[4:8], sems[8:12]
     over_s, over_r, back_s, back_r, own_sem = sems[12:17]
-    x_s, x_r, g_s, g_r, load_sem, store_sem, seq_s, seq_r = sems[17:]
+    x_s, x_r, g_s, g_r, load_sem, store_sem, seq_s, seq_r, turn_sem = sems[17:]
     segments = lax.axis_size("segment")
     members = lax.axis_size("dp")
     seg = lax.axis_index("segment")
@@ -243,7 +243,10 @@
         for h in range(2):
             go_over(h).start()
 
-    @pl.when(jnp.logical_not(closing))
+    shared = seg >= 2
+    later = shared & (lax.rem(seg, 2) == 1)
+
+    @pl.when(jnp.logical_not(closing) & jnp.logical_not(later))
     def _():
         start_own()
 
@@ -270,6 +273,7 @@
         for h in range(2):
             go_over(h).wait_recv()
         visit.open()
+        pl.when(jnp.logical_not(later))(start_own)
         for h in range(2):
             visit.arrived_first(h)
         for h in range(2):
@@ -282,7 +286,6 @@
         for h in range(2):
             visit.first_done(h)
             visit.spread(h, 3)
-        start_own()
         for i in range(4):
             for h in range(2):
                 if i > 0:
@@ -338,8 +341,18 @@
         getattr(main, step)(*which)
         on_all_but_opening(lambda: getattr(rest, step)(*which))
 
+    @pl.when(later)
+    def _():
+        pl.semaphore_wait(turn_sem, 1)
+        start_own()
+
     for h in range(2):
         everywhere("arrived_first", h)
+
+    @pl.when(shared & jnp.logical_not(later))
+    def _():
+        pl.semaphore_signal(turn_sem, inc=1, device_id=(lax.rem(seg + 1, segments), me), device_id_type=MESH)
+
     for h in range(2):
         everywhere("spread", h, 1)
         everywhere("spread", h, 2)
@@ -615,7 +628,7 @@
             *((dma((2, 4)), dma((2, 4)), dma((2, 4, 4)), dma((2, 4, 4))) * 3),
             dma((2,)), dma((2,)), dma((2, 16)), dma((2, 16)), dma((2,)),
             dma((micro, CHUNKS)), dma((micro, CHUNKS)), dma((micro, CHUNKS)), dma((micro, CHUNKS)),
-            dma((3,)), dma((2 * micro,)), dma((members,)), dma((members,)),
+            dma((3,)), dma((2 * micro,)), dma((members,)), dma((members,)), pltpu.SemaphoreType.REGULAR,
         ],
         compiler_params=pltpu.CompilerParams(
             collective_id=0, has_side_effects=True, vmem_limit_bytes=60 * 1024 * 1024

time: 339 us -> 333 us (0.982)
  Pallas kernels: 332 us -> 326 us
    pallas_call x1, Pallas kernels: 332 us -> 326 us  [shards(): pl.pallas_call(kernel, out_shape=(stream, stream, grad, grad), in_specs=[...]
where the time goes in v4:
time: 333 us; the launch traced here: 332 us
  Pallas kernels  326 us (98%)
  local copies, waits for them, and re-layouts  5.92 us (2%)
    pallas_call x1, Pallas kernels, shards(): pl.pallas_call(kernel, out_shape=(stream, stream, grad, grad), in_specs=[...  326 us

profile of v4, /device:TPU:0, one launch (start us, length us, event | category | flops | bytes accessed | tf_op | source)
XLA Modules:
  0.0 332.5 jit_solution(6262889431897256288)
XLA Ops:
  0.6 325.9 %shard_map.120 = (bf16[2,128,4096]{2,1,0:T(8,128)(2,1)}, bf16[2,128,4096]{2,1,0:T(8,128)(2,1)}, f32[16,8,256]{2,1,0:T(8,128)}, f32[16,8,256]{2,1,0:T(8,128)}) custom-call(bf16[2,128,4096]{2,1,0:T(8,128)(2,1)} %bitcast.16, bf16[256,4096]{1,0:T(8,128)(2,1)} %bitcast.17, f32[1,4096]{1,0:T(1,128)} %gain.1, bf16[16,8,4096]{2,1,0:T(8,128)(2,1)} %bitcast.19, ...), custom_call_target="tpu_custom_call" | custom-call | tf_op jit(solution)/shard_map/pallas_call | solution.py:609
  326.5 0.0 copy-start
  326.6 3.3 copy.19
  329.8 0.0 copy-done
  329.8 0.0 copy-start.2
  329.8 0.0 copy-start.1
  329.8 1.3 copy.20
  331.2 0.0 copy-done.2
  331.2 0.7 copy.21
  331.8 0.0 copy-done.1
  331.8 0.7 copy.22
Async XLA Ops:
  326.5 3.3 copy-start
  329.8 1.3 copy-start.2
  329.8 2.0 copy-start.1

commit v5 on v4

--- a/solution.py
+++ b/solution.py
@@ -56,8 +56,13 @@
     def chunk(q):
         return pl.ds(pl.multiple_of(q * wide, wide), wide)
 
-    def by_columns(q):
-        return wbuf[q // (CHUNKS // 2), :, chunk(lax.rem(q, CHUNKS // 2))]
+    def columns_of(q, at_once):
+        size = at_once * wide
+        return pl.ds(pl.multiple_of(q * size, size), size)
+
+    def by_columns(q, at_once=1):
+        count = half // (at_once * wide)
+        return wbuf[q // count, :, columns_of(lax.rem(q, count), at_once)]
 
     def hop(buf, target, m, q, s, r, to):
         return pltpu.make_async_remote_copy(
@@ -121,18 +126,22 @@
         inv = invbuf[m]
         low = lowbuf[m]
 
+        at_once = 2 if kind == "wide" else 1
+
         def give_out(q, c):
-            total = dot(hbuf[m], by_columns(q)) if kind == "columns" else acc[m, :, chunk(q)]
-            total = xbuf[m, :, chunk(q)].astype(F32) + inv * total + dot(low, up[m, :, chunk(q)])
-            obuf[m, :, chunk(q)] = total.astype(BF16)
-
-            @pl.when(seg < last)
-            def _():
-                onward(m, q).start()
+            cols = columns_of(q, at_once)
+            total = dot(hbuf[m], by_columns(q, at_once)) if kind in ("columns", "wide") else acc[m, :, cols]
+            total = xbuf[m, :, cols].astype(F32) + inv * total + dot(low, up[m, :, cols])
+            obuf[m, :, cols] = total.astype(BF16)
+            if kind != "wide":
+
+                @pl.when(seg < last)
+                def _():
+                    onward(m, q).start()
 
             return c
 
-        over_chunks(give_out)
+        lax.fori_loop(0, CHUNKS // at_once, give_out, 0)
         pltpu.make_async_copy(obuf.at[m], hidden.at[m], store_sem.at[m]).start()
 
     def forward(m, kind):
@@ -444,27 +453,26 @@
                     acc[m, :, i * half : (i + 1) * half] += dot(g, wbuf[i, chunk(q), :])
             change = obuf[m, :, chunk(q)].astype(F32) - xbuf[m, :, chunk(q)].astype(F32)
             along = along + jnp.sum(g.astype(F32) * change, axis=1, keepdims=True)
+            if kind == "rows":
+                return along, gl
             return along, gl + dot(g, up[m, :, chunk(q)], ((1,), (1,)))
 
         along, gl = over_chunks(take_in, (column, narrow))
-        glow = gl.astype(BF16)
-        glowbuf[m] = glow
+        if kind != "rows":
+            glowbuf[m] = gl.astype(BF16)
+        glow = glowbuf[m]
         inv = invbuf[m]
         coef = along / width * inv * inv
         if between is not None:
-
-            @pl.when(seg == 0)
-            def _():
-                between(m)
-
-        at_once = 2 if kind == "rows" else 1
+            between(m)
+        at_once = 2 if kind in ("rows", "wide") else 1
 
         def give_out(q, c):
-            cols = pl.ds(pl.multiple_of(q * at_once * wide, at_once * wide), at_once * wide)
+            cols = columns_of(q, at_once)
             if kind == "comes":
                 dh = acc[m, :, cols]
-            elif kind == "columns":
-                dh = dot(gbuf[m], by_columns(q))
+            elif kind in ("columns", "wide"):
+                dh = dot(gbuf[m], by_columns(q, at_once))
             else:
                 turned = dot(wbuf[0, cols, :], gbuf[m, :, :half], ((1,), (1,)))
                 turned = turned + dot(wbuf[1, cols, :], gbuf[m, :, half:], ((1,), (1,)))
@@ -524,19 +532,27 @@
         def _():
             share_all()
 
-    @pl.when(even)
-    def _():
-        each_micro(lambda m: backward(m, "columns", before_the_last))
+    def and_grads(m, kind):
+        backward(m, kind)
+        adapter_grads(m)
+
+    @pl.when(seg == 0)
+    def _():
+        each_micro(lambda m: backward(m, "wide", before_the_last))
+
+    @pl.when(even & (seg > 0))
+    def _():
+        each_micro(lambda m: and_grads(m, "columns"))
 
     @pl.when(jnp.logical_not(even) & (seg < last))
     def _():
-        each_micro(lambda m: backward(m, "comes"))
+        each_micro(lambda m: and_grads(m, "comes"))
 
     @pl.when(seg == last)
     def _():
         pltpu.make_async_copy(cot, gbuf, load_sem.at[1]).wait()
 
-        def both(m):
+        def ready(m):
             keep = lax.broadcasted_iota(jnp.int32, (rows, wide), 0) < lens[m, me]
 
             def masked(q, c):
@@ -544,15 +560,19 @@
                 return c
 
             over_chunks(masked)
-            forward(m, "columns")
+            glowbuf[m] = dot(gbuf[m], up[m], ((1,), (1,))).astype(BF16)
+
+        def both(m):
+            forward(m, "wide")
             backward(m, "rows")
 
+        each_micro(ready)
         each_micro(both)
         each_micro(normed)
+        each_micro(adapter_grads)
 
     @pl.when(seg > 0)
     def _():
-        each_micro(adapter_grads)
         share_all()
 
     def add(mine, source, fresh):

time: 333 us -> 331 us (level)
  no operation moved by 1% of the time
where the time goes in v5:
time: 331 us
  Pallas kernels  324 us (98%)
  local copies, waits for them, and re-layouts  5.92 us (2%)
    pallas_call x1, Pallas kernels, shards(): pl.pallas_call(kernel, out_shape=(stream, stream, grad, grad), in_specs=[...  324 us

profile of v5, /device:TPU:0, one launch (start us, length us, event | category | flops | bytes accessed | tf_op | source)
XLA Modules:
  0.0 330.6 jit_solution(8334393842735037666)
XLA Ops:
  0.6 324.0 %shard_map.120 = (bf16[2,128,4096]{2,1,0:T(8,128)(2,1)}, bf16[2,128,4096]{2,1,0:T(8,128)(2,1)}, f32[16,8,256]{2,1,0:T(8,128)}, f32[16,8,256]{2,1,0:T(8,128)}) custom-call(bf16[2,128,4096]{2,1,0:T(8,128)(2,1)} %bitcast.16, bf16[256,4096]{1,0:T(8,128)(2,1)} %bitcast.17, f32[1,4096]{1,0:T(1,128)} %gain.1, bf16[16,8,4096]{2,1,0:T(8,128)(2,1)} %bitcast.19, ...), custom_call_target="tpu_custom_call" | custom-call | tf_op jit(solution)/shard_map/pallas_call | solution.py:629
  324.7 0.0 copy-start
  324.7 3.3 copy.19
  327.9 0.0 copy-done
  327.9 0.0 copy-start.2
  327.9 0.0 copy-start.1
  327.9 1.3 copy.20
  329.3 0.0 copy-done.2
  329.3 0.7 copy.21
  329.9 0.0 copy-done.1
  329.9 0.7 copy.22
Async XLA Ops:
  324.7 3.3 copy-start
  327.9 1.3 copy-start.2
  327.9 2.0 copy-start.1

commit v6 on v5

--- a/solution.py
+++ b/solution.py
@@ -64,9 +64,10 @@
         count = half // (at_once * wide)
         return wbuf[q // count, :, columns_of(lax.rem(q, count), at_once)]
 
-    def hop(buf, target, m, q, s, r, to):
+    def hop(buf, target, m, q, size, s, r, to):
+        cols = columns_of(q, size)
         return pltpu.make_async_remote_copy(
-            src_ref=buf.at[m, :, chunk(q)], dst_ref=target.at[m, :, chunk(q)], send_sem=s.at[m, q], recv_sem=r.at[m, q],
+            src_ref=buf.at[m, :, cols], dst_ref=target.at[m, :, cols], send_sem=s.at[m, q], recv_sem=r.at[m, q],
             device_id=(to, me), device_id_type=MESH,
         )
 
@@ -100,24 +101,23 @@
         if kind == "comes":
             acc[m] = jnp.zeros((rows, width), F32)
 
+        size = 2 if kind in ("columns", "wide") else 1
+
         def take_in(q, c):
             ss, lw = c
             if kind != "early":
-
-                @pl.when(seg > 0)
-                def _():
-                    onward(m, q).wait_recv()
-
-            v = xbuf[m, :, chunk(q)].astype(F32)
-            h = (v * gain[:, chunk(q)]).astype(BF16)
+                onward(m, q, size).wait_recv()
+            cols = columns_of(q, size)
+            v = xbuf[m, :, cols].astype(F32)
+            h = (v * gain[:, cols]).astype(BF16)
             if kind == "comes":
                 for i in range(2):
-                    acc[m, :, i * half : (i + 1) * half] += dot(h, wbuf[i, chunk(q), :])
+                    acc[m, :, i * half : (i + 1) * half] += dot(h, wbuf[i, cols, :])
             else:
-                hbuf[m, :, chunk(q)] = h
-            return ss + jnp.sum(v * v, axis=1, keepdims=True), lw + dot(h, down[m, :, chunk(q)], ((1,), (1,)))
-
-        ss, lw = over_chunks(take_in, (column, narrow))
+                hbuf[m, :, cols] = h
+            return ss + jnp.sum(v * v, axis=1, keepdims=True), lw + dot(h, down[m, :, cols], ((1,), (1,)))
+
+        ss, lw = lax.fori_loop(0, CHUNKS // size, take_in, (column, narrow))
         inv = lax.rsqrt(ss / width + EPS)
         invbuf[m] = inv
         lowbuf[m] = (lw * inv).astype(BF16)
@@ -126,7 +126,7 @@
         inv = invbuf[m]
         low = lowbuf[m]
 
-        at_once = 2 if kind == "wide" else 1
+        at_once = 1 if kind == "columns" else 2
 
         def give_out(q, c):
             cols = columns_of(q, at_once)
@@ -134,11 +134,7 @@
             total = xbuf[m, :, cols].astype(F32) + inv * total + dot(low, up[m, :, cols])
             obuf[m, :, cols] = total.astype(BF16)
             if kind != "wide":
-
-                @pl.when(seg < last)
-                def _():
-                    onward(m, q).start()
-
+                onward(m, q, at_once).start()
             return c
 
         lax.fori_loop(0, CHUNKS // at_once, give_out, 0)
@@ -307,6 +303,19 @@
             for h in range(2):
                 visit.second_done(h, i)
                 come_back(h, i, 3).start()
+
+    def everywhere(step, *which):
+        getattr(main, step)(*which)
+        on_all_but_opening(lambda: getattr(rest, step)(*which))
+
+    @pl.when(jnp.logical_not(later))
+    def _():
+        for h in range(2):
+            everywhere("arrived_first", h)
+
+    @pl.when(shared & jnp.logical_not(later))
+    def _():
+        pl.semaphore_signal(turn_sem, inc=1, device_id=(lax.rem(seg + 1, segments), me), device_id_type=MESH)
 
     pltpu.make_async_copy(alloc, table, load_sem.at[2]).wait()
     known = table[...].astype(F32).astype(BF16)
@@ -330,6 +339,13 @@
 
     lax.fori_loop(0, width // step, adapters, 0)
 
+    @pl.when(later)
+    def _():
+        pl.semaphore_wait(turn_sem, 1)
+        start_own()
+        for h in range(2):
+            everywhere("arrived_first", h)
+
     @pl.when(seg == 0)
     def _():
         pltpu.make_async_copy(emb, xbuf, load_sem.at[0]).wait()
@@ -345,22 +361,6 @@
                     acc[m, :, h * half : h * half + most] += dot(
                         hbuf[m, :, pl.ds(start, block)], wbuf[h, pl.ds(start, block), :most]
                     )
-
-    def everywhere(step, *which):
-        getattr(main, step)(*which)
-        on_all_but_opening(lambda: getattr(rest, step)(*which))
-
-    @pl.when(later)
-    def _():
-        pl.semaphore_wait(turn_sem, 1)
-        start_own()
-
-    for h in range(2):
-        everywhere("arrived_first", h)
-
-    @pl.when(shared & jnp.logical_not(later))
-    def _():
-        pl.semaphore_signal(turn_sem, inc=1, device_id=(lax.rem(seg + 1, segments), me), device_id_type=MESH)
 
     for h in range(2):
         everywhere("spread", h, 1)
@@ -443,21 +443,24 @@
         if kind == "comes":
             acc[m] = jnp.zeros((rows, width), F32)
 
+        size = 1 if kind == "comes" else 2
+
         def take_in(q, c):
             along, gl = c
             if kind != "rows":
-                back(m, q).wait_recv()
-            g = gbuf[m, :, chunk(q)]
+                back(m, q, size).wait_recv()
+            cols = columns_of(q, size)
+            g = gbuf[m, :, cols]
             if kind == "comes":
                 for i in range(2):
-                    acc[m, :, i * half : (i + 1) * half] += dot(g, wbuf[i, chunk(q), :])
-            change = obuf[m, :, chunk(q)].astype(F32) - xbuf[m, :, chunk(q)].astype(F32)
+                    acc[m, :, i * half : (i + 1) * half] += dot(g, wbuf[i, cols, :])
+            change = obuf[m, :, cols].astype(F32) - xbuf[m, :, cols].astype(F32)
             along = along + jnp.sum(g.astype(F32) * change, axis=1, keepdims=True)
             if kind == "rows":
                 return along, gl
-            return along, gl + dot(g, up[m, :, chunk(q)], ((1,), (1,)))
-
-        along, gl = over_chunks(take_in, (column, narrow))
+            return along, gl + dot(g, up[m, :, cols], ((1,), (1,)))
+
+        along, gl = lax.fori_loop(0, CHUNKS // size, take_in, (column, narrow))
         if kind != "rows":
             glowbuf[m] = gl.astype(BF16)
         glow = glowbuf[m]
@@ -465,7 +468,7 @@
         coef = along / width * inv * inv
         if between is not None:
             between(m)
-        at_once = 2 if kind in ("rows", "wide") else 1
+        at_once = 1 if kind == "columns" else 2
 
         def give_out(q, c):
             cols = columns_of(q, at_once)
@@ -481,11 +484,8 @@
             out = gbuf[m, :, cols].astype(F32) + inv * (gain[:, cols] * dh)
             gout[m, :, cols] = (out - xbuf[m, :, cols].astype(F32) * coef).astype(BF16)
 
-            @pl.when(seg > 0)
-            def _():
-                for i in range(at_once):
-                    back(m, q * at_once + i).start()
-
+            if kind != "wide":
+                back(m, q, at_once).start()
             return c
 
         lax.fori_loop(0, CHUNKS // at_once, give_out, 0)
@@ -601,17 +601,26 @@
         pltpu.make_async_copy(obuf.at[m], hidden.at[m], store_sem.at[m]).wait()
         pltpu.make_async_copy(gout.at[m], grads_in.at[m], store_sem.at[micro + m]).wait()
 
-    @pl.when(seg < last)
-    def _():
+    def all_sent(copy, size):
         for m in range(micro):
-            for q in range(CHUNKS):
-                onward(m, q).wait_send()
-
-    @pl.when(seg > 0)
-    def _():
-        for m in range(micro):
-            for q in range(CHUNKS):
-                back(m, q).wait_send()
+            for q in range(CHUNKS // size):
+                copy(m, q, size).wait_send()
+
+    @pl.when(even)
+    def _():
+        all_sent(onward, 2)
+
+    @pl.when(even & (seg > 0))
+    def _():
+        all_sent(back, 1)
+
+    @pl.when(jnp.logical_not(even))
+    def _():
+        all_sent(back, 2)
+
+    @pl.when(jnp.logical_not(even) & (seg < last))
+    def _():
+        all_sent(onward, 1)
 
 
 def shards(embeds, base_weight, norm_gain, skill_down, skill_up, task_ids, allocation, target_lengths, cotangent):

time: 331 us -> 329 us (level)
  no operation moved by 1% of the time
where the time goes in v6:
time: 329 us
  Pallas kernels  322 us (98%)
  local copies, waits for them, and re-layouts  5.92 us (2%)
    pallas_call x1, Pallas kernels, shards(): pl.pallas_call(kernel, out_shape=(stream, stream, grad, grad), in_specs=[...  322 us

profile of v6, /device:TPU:0, one launch (start us, length us, event | category | flops | bytes accessed | tf_op | source)
XLA Modules:
  0.0 328.8 jit_solution(7987228820323965173)
XLA Ops:
  0.6 322.2 %shard_map.120 = (bf16[2,128,4096]{2,1,0:T(8,128)(2,1)}, bf16[2,128,4096]{2,1,0:T(8,128)(2,1)}, f32[16,8,256]{2,1,0:T(8,128)}, f32[16,8,256]{2,1,0:T(8,128)}) custom-call(bf16[2,128,4096]{2,1,0:T(8,128)(2,1)} %bitcast.16, bf16[256,4096]{1,0:T(8,128)(2,1)} %bitcast.17, f32[1,4096]{1,0:T(1,128)} %gain.1, bf16[16,8,4096]{2,1,0:T(8,128)(2,1)} %bitcast.19, ...), custom_call_target="tpu_custom_call" | custom-call | tf_op jit(solution)/shard_map/pallas_call | solution.py:638
  322.8 0.0 copy-start
  322.9 3.3 copy.19
  326.1 0.0 copy-done
  326.1 0.0 copy-start.2
  326.1 0.0 copy-start.1
  326.1 1.3 copy.20
  327.5 0.0 copy-done.2
  327.5 0.7 copy.21
  328.1 0.0 copy-done.1
  328.1 0.7 copy.22
Async XLA Ops:
  322.8 3.3 %copy-start = (bf16[2,128,4096]{2,1,0:T(8,128)(2,1)S(1)}, bf16[2,128,4096]{2,1,0:T(8,128)(2,1)}, u32[]{:S(2)}) copy-start(bf16[2,128,4096]{2,1,0:T(8,128)(2,1)} %get-tuple-element.9) | copy-start | bytes 6291460
  326.1 1.3 copy-start.2
  326.1 2.0 copy-start.1

commit v7 on v6

--- a/solution.py
+++ b/solution.py
@@ -64,6 +64,11 @@
         count = half // (at_once * wide)
         return wbuf[q // count, :, columns_of(lax.rem(q, count), at_once)]
 
+    def last_of(buf, m, q, at_once):
+        count = half // (at_once * wide)
+        final = pl.ds(width - wide, wide)
+        return dot(buf[m, :, final], wbuf[q // count, final, columns_of(lax.rem(q, count), at_once)])
+
     def hop(buf, target, m, q, size, s, r, to):
         cols = columns_of(q, size)
         return pltpu.make_async_remote_copy(
@@ -110,11 +115,14 @@
             cols = columns_of(q, size)
             v = xbuf[m, :, cols].astype(F32)
             h = (v * gain[:, cols]).astype(BF16)
+            hbuf[m, :, cols] = h
             if kind == "comes":
-                for i in range(2):
-                    acc[m, :, i * half : (i + 1) * half] += dot(h, wbuf[i, cols, :])
-            else:
-                hbuf[m, :, cols] = h
+
+                @pl.when(q < CHUNKS - 1)
+                def _():
+                    for i in range(2):
+                        acc[m, :, i * half : (i + 1) * half] += dot(h, wbuf[i, cols, :])
+
             return ss + jnp.sum(v * v, axis=1, keepdims=True), lw + dot(h, down[m, :, cols], ((1,), (1,)))
 
         ss, lw = lax.fori_loop(0, CHUNKS // size, take_in, (column, narrow))
@@ -126,11 +134,13 @@
         inv = invbuf[m]
         low = lowbuf[m]
 
-        at_once = 1 if kind == "columns" else 2
+        at_once = {"columns": 1, "wide": 4}.get(kind, 2)
 
         def give_out(q, c):
             cols = columns_of(q, at_once)
             total = dot(hbuf[m], by_columns(q, at_once)) if kind in ("columns", "wide") else acc[m, :, cols]
+            if kind == "comes":
+                total = total + last_of(hbuf, m, q, at_once)
             total = xbuf[m, :, cols].astype(F32) + inv * total + dot(low, up[m, :, cols])
             obuf[m, :, cols] = total.astype(BF16)
             if kind != "wide":
@@ -452,8 +462,12 @@
             cols = columns_of(q, size)
             g = gbuf[m, :, cols]
             if kind == "comes":
-                for i in range(2):
-                    acc[m, :, i * half : (i + 1) * half] += dot(g, wbuf[i, cols, :])
+
+                @pl.when(q < CHUNKS - 1)
+                def _():
+                    for i in range(2):
+                        acc[m, :, i * half : (i + 1) * half] += dot(g, wbuf[i, cols, :])
+
             change = obuf[m, :, cols].astype(F32) - xbuf[m, :, cols].astype(F32)
             along = along + jnp.sum(g.astype(F32) * change, axis=1, keepdims=True)
             if kind == "rows":
@@ -468,12 +482,12 @@
         coef = along / width * inv * inv
         if between is not None:
             between(m)
-        at_once = 1 if kind == "columns" else 2
+        at_once = {"columns": 1, "wide": 4}.get(kind, 2)
 
         def give_out(q, c):
             cols = columns_of(q, at_once)
             if kind == "comes":
-                dh = acc[m, :, cols]
+                dh = acc[m, :, cols] + last_of(gbuf, m, q, at_once)
             elif kind in ("columns", "wide"):
                 dh = dot(gbuf[m], by_columns(q, at_once))
             else:

time: 329 us -> 329 us (level)
  no operation moved by 1% of the time
where the time goes in v7:
time: 329 us
  Pallas kernels  322 us (98%)
  local copies, waits for them, and re-layouts  5.92 us (2%)
    pallas_call x1, Pallas kernels, shards(): pl.pallas_call(kernel, out_shape=(stream, stream, grad, grad), in_specs=[...  322 us

profile of v7, /device:TPU:0, one launch (start us, length us, event | category | flops | bytes accessed | tf_op | source)
XLA Modules:
  0.0 328.6 jit_solution(8201947692208809436)
XLA Ops:
  0.6 322.0 %shard_map.120 = (bf16[2,128,4096]{2,1,0:T(8,128)(2,1)}, bf16[2,128,4096]{2,1,0:T(8,128)(2,1)}, f32[16,8,256]{2,1,0:T(8,128)}, f32[16,8,256]{2,1,0:T(8,128)}) custom-call(bf16[2,128,4096]{2,1,0:T(8,128)(2,1)} %bitcast.16, bf16[256,4096]{1,0:T(8,128)(2,1)} %bitcast.17, f32[1,4096]{1,0:T(1,128)} %gain.1, bf16[16,8,4096]{2,1,0:T(8,128)(2,1)} %bitcast.19, ...), custom_call_target="tpu_custom_call" | custom-call | tf_op jit(solution)/shard_map/pallas_call | solution.py:652
  322.7 0.0 copy-start
  322.7 3.3 copy.19
  326.0 0.0 copy-done
  326.0 0.0 copy-start.2
  326.0 0.0 copy-start.1
  326.0 1.3 copy.20
  327.3 0.0 copy-done.2
  327.3 0.7 copy.21
  328.0 0.0 copy-done.1
  328.0 0.7 copy.22
Async XLA Ops:
  322.7 3.3 %copy-start = (bf16[2,128,4096]{2,1,0:T(8,128)(2,1)S(1)}, bf16[2,128,4096]{2,1,0:T(8,128)(2,1)}, u32[]{:S(2)}) copy-start(bf16[2,128,4096]{2,1,0:T(8,128)(2,1)} %get-tuple-element.9) | copy-start | bytes 6291460
  326.0 1.3 copy-start.2
  326.0 2.0 copy-start.1
